TPU v7x, 32 devices: a whole 2x2x4 slice. The times are simulated.
32 devices in a mesh: grp: 2 (over x), gx: 16 (over z, y, core).
Axes of the slice: x: 2, y: 2, z: 4, core: 2. Of those that a mesh axis runs over, the one named last changes fastest.
Arguments:
- tensor: float32 [128, 1152, 576], P(('grp', 'gx')), parts along dimension 0, may hold values from -6 to 6
- factor_b: float32 [2304, 256], P('grp'), parts along dimension 0, may hold values from -7 to 7
- factor_c: float32 [1152, 256], P('grp'), parts along dimension 0, may hold values from -7 to 7
Outputs:
- new_a: float32 [128, 256], P(('grp', 'gx')), parts along dimension 0
- new_b: float32 [2304, 256], P(('grp', 'gx')), parts along dimension 0
- new_c: float32 [1152, 256], P(('grp', 'gx')), parts along dimension 0
There are 2 independent parts, one for each index of `grp`. A program takes and returns all parts, laid end to end along the dimension named above; each array names one. Nothing has to cross between parts.
All inputs are finite; a program needn't handle non-finite values.
Results may differ from a plain program's by a relative error of at most 0.0003.
Values sent between devices are 32-bit elements; how exact they have to be, the bound alone decides.
No kernel may reach another device: no remote copies, remote signals or barrier semaphores. Data moves between devices by JAX's collectives and lax.ppermute only.
A program may use at most 64 MiB of HBM per device.

v0:
```python
import functools

import jax
import jax.numpy as jnp
from jax import lax
from jax.experimental import pallas as pl
from jax.experimental.pallas import tpu as pltpu
from jax.sharding import PartitionSpec as P

HIGH = lax.Precision.HIGHEST
PANEL = 32
LIMIT = 50 * 1024 * 1024
SMALL = 8 * 1024 * 1024


def dot(a, b):
    return jnp.dot(a, b, precision=HIGH, preferred_element_type=jnp.float32)


def dot_first(a, b):
    return lax.dot_general(
        a, b, (((0,), (0,)), ((), ())), precision=HIGH, preferred_element_type=jnp.float32
    )


def split(x):
    high = x.astype(jnp.bfloat16)
    low = (x - high.astype(jnp.float32)).astype(jnp.bfloat16)
    return high, low


def split3(x):
    high = x.astype(jnp.bfloat16)
    rest = x - high.astype(jnp.float32)
    mid = rest.astype(jnp.bfloat16)
    return high, mid, (rest - mid.astype(jnp.float32)).astype(jnp.bfloat16)


def mul(a, b):
    return jnp.dot(a, b, preferred_element_type=jnp.float32)


def mul3(a, b):
    a_high, a_low = split(a)
    b_high, b_low = split(b)
    return mul(a_high, b_high) + (mul(a_low, b_high) + mul(a_high, b_low))


def eye_mask(size):
    return lax.broadcasted_iota(jnp.int32, (size, size), 0) == lax.broadcasted_iota(
        jnp.int32, (size, size), 1
    )


def system(first, second):
    size = first.shape[0]
    product = first * second
    diagonal = jnp.where(eye_mask(size), product, 0.0)
    mean = jnp.sum(diagonal) / size
    return product * (1.0 / mean) + jnp.where(eye_mask(size), 0.1, 0.0), mean


def reciprocal(x):
    guess = pl.reciprocal(x, approx=True)
    guess = guess * (2.0 - x * guess)
    return guess * (2.0 - x * guess)


def spread(x, row):
    return jnp.broadcast_to(x[row : row + 1, :], (8, 128))


def eliminate(ref):
    size = ref.shape[0]
    tiles = size // 128
    groups = PANEL // 8
    lane = lax.broadcasted_iota(jnp.int32, (8, 128), 1)
    sub = lax.broadcasted_iota(jnp.int32, (8, 128), 0)
    for start in range(0, size, PANEL):
        before = ref[start : start + PANEL, :]
        rows = [
            [ref[start + 8 * t : start + 8 * t + 8, 128 * h : 128 * h + 128] for h in range(tiles)]
            for t in range(groups)
        ]
        for q in range(groups):
            column = start + 8 * q
            home, offset = column // 128, column % 128
            cols = [
                [
                    jnp.broadcast_to(rows[t][home][:, offset + k : offset + k + 1], (8, 128))
                    for k in range(8)
                ]
                for t in range(groups)
            ]
            for k in range(0, 8, 2):
                one, two = cols[q][k], cols[q][k + 1]
                a, b, c, d = spread(one, k), spread(two, k), spread(one, k + 1), spread(two, k + 1)
                inverse = reciprocal(a * d - b * c)
                is_one, is_two = sub == k, sub == k + 1
                for j in range(k + 2, 8):
                    upper, lower = spread(cols[q][j], k), spread(cols[q][j], k + 1)
                    first_row = d * upper - b * lower
                    second_row = a * lower - c * upper
                    for t in range(groups):
                        change = cols[t][k] * first_row + cols[t][k + 1] * second_row
                        fresh = cols[t][j] - change * inverse
                        if t == q:
                            fresh = jnp.where(is_one, first_row * inverse, fresh)
                            fresh = jnp.where(is_two, second_row * inverse, fresh)
                        cols[t][j] = fresh
                p11, p12, p21, p22 = d * inverse, b * inverse, c * inverse, a * inverse
                on_one, on_two = lane == offset + k, lane == offset + k + 1
                for h in range(tiles):
                    upper, lower = spread(rows[q][h], k), spread(rows[q][h], k + 1)
                    if h == home:
                        upper = jnp.where(on_two, 0.0, jnp.where(on_one, 1.0, upper))
                        lower = jnp.where(on_one, 0.0, jnp.where(on_two, 1.0, lower))
                    first_row = p11 * upper - p12 * lower
                    second_row = p22 * lower - p21 * upper
                    for t in range(groups):
                        base = rows[t][h]
                        if h == home:
                            base = jnp.where(on_one | on_two, 0.0, base)
                        fresh = base - (cols[t][k] * first_row + cols[t][k + 1] * second_row)
                        if t == q:
                            fresh = jnp.where(is_one, first_row, fresh)
                            fresh = jnp.where(is_two, second_row, fresh)
                        rows[t][h] = fresh
                yield
        solved = jnp.concatenate([jnp.concatenate(group, axis=1) for group in rows], axis=0)
        wide = lax.broadcasted_iota(jnp.int32, (PANEL, size), 1)
        inside = (wide >= start) & (wide < start + PANEL)
        factor = jnp.where(inside, 0.0, jnp.where(wide < start, -before, before))
        fh, fm, fl = split3(factor)
        sh, sm, sl = split3(solved)
        change = lax.dot_general(
            jnp.concatenate([fh, fh, fh, fm, fm, fl], axis=0),
            jnp.concatenate([sh, sm, sl, sh, sm, sh], axis=0),
            (((0,), (0,)), ((), ())),
            preferred_element_type=jnp.float32,
        )
        tall = lax.broadcasted_iota(jnp.int32, (size, 128), 1)
        for h in range(tiles):
            base = ref[:, 128 * h : 128 * h + 128]
            if h == start // 128:
                offset = start % 128
                base = jnp.where((tall >= offset) & (tall < offset + PANEL), 0.0, base)
            ref[:, 128 * h : 128 * h + 128] = base - change[:, 128 * h : 128 * h + 128]
        ref[start : start + PANEL, :] = solved
        yield


def invert(ref):
    for _ in eliminate(ref):
        pass


def chunks(total, most):
    return [(at, min(most, total - at)) for at in range(0, total, most)]


def fetch(x_hbm, x_ref, sems):
    copies = [
        pltpu.make_async_copy(x_hbm.at[i], x_ref.at[i], sems.at[i]) for i in range(x_ref.shape[0])
    ]
    for copy in copies:
        copy.start()
    return copies


def weave(first, second, total_first, total_second):
    taken = 0
    for n in range(total_first):
        next(first, None)
        while taken * total_first < (n + 1) * total_second:
            next(second, None)
            taken += 1
    for generator in (first, second):
        for _ in generator:
            pass


def contract(x_ref, stack, turned, out, sums, partial):
    count, _, width = x_ref.shape
    rank = out.shape[1]
    lane = lax.broadcasted_iota(jnp.int32, (rank, 128), 1)
    for i in range(count):
        for at, size in chunks(width, 256):
            high, low = split(x_ref[i, :, at : at + size])
            both = mul(stack[...], high)
            block = both[:rank] + (both[rank:] + mul(stack[:rank], low))
            out[i, :, at : at + size] = block
            block = block * turned[:, at : at + size]
            total = block[:, :128]
            for h in range(128, size, 128):
                total = total + block[:, h : h + 128]
            partial[...] = total if at == 0 else partial[...] + total
            yield
        sums[...] = jnp.where(lane == i, jnp.sum(partial[...], axis=1, keepdims=True), sums[...])


def first_kernel(
    x_hbm, b_ref, c_ref, raw_ref, keep_ref, send_ref, gram_ref, x_ref, inv, out, turned, stack, sums, partial, sems
):
    copies = fetch(x_hbm, x_ref, sems)
    count, _, width = x_ref.shape
    rank = inv.shape[0]
    half = rank // 2
    c = c_ref[...]
    c_turned = c.T
    stack[:rank], stack[rank:] = split(c_turned)
    gram_c = mul3(c_turned, c)
    gram_ref[...] = gram_c
    turned[...] = b_ref[...].T
    matrix, mean = system(mul3(turned[...], b_ref[...]), gram_c)
    inv[...] = matrix
    sums[...] = jnp.zeros_like(sums)
    for copy in copies:
        copy.wait()
    weave(
        eliminate(inv),
        contract(x_ref, stack, turned, out, sums, partial),
        (rank // PANEL) * (PANEL // 2 + 1),
        count * len(chunks(width, 256)),
    )
    raw = dot(inv[...], sums[...]) * (1.0 / mean)
    raw_rows = raw.T[:count, :]
    raw_ref[...] = raw_rows
    sums[...] = raw
    core = lax.axis_index("gx") & 1
    members, rows, _ = keep_ref.shape
    pieces = [
        jnp.where(core == c, raw_rows[i : i + 1, 128 * h : 128 * h + 128], 0.0)
        for c in range(2)
        for h in range(rank // 128)
        for i in range(count)
    ]
    tail = jnp.concatenate(
        [jnp.concatenate(pieces[at : at + rows], axis=0) for at in range(0, len(pieces), rows)], axis=1
    )
    for ref, place in ((send_ref, 1 - core), (keep_ref, core)):
        group = max(rows, 8)
        for at in range(0, half, group):
            here = pl.ds(pl.multiple_of(place * half, half) + at, group)
            scale = sums[here, :]
            total = out[0, here, :] * scale[:, 0:1]
            for i in range(1, count):
                total = total + out[i, here, :] * scale[:, i : i + 1]
            for n in range(group // rows):
                ref[at // rows + n, :, :width] = total[n * rows : (n + 1) * rows, :]
                ref[at // rows + n, :, width:] = tail


def first_call(turned, factor_b, factor_c, devices):
    count, depth, width = turned.shape
    rank = factor_b.shape[1]
    vmem = pl.BlockSpec(memory_space=pltpu.VMEM)
    part = jax.ShapeDtypeStruct(
        (devices // 2, rank // devices, width + 2 * count * devices), jnp.float32
    )
    return pl.pallas_call(
        first_kernel,
        in_specs=[pl.BlockSpec(memory_space=pltpu.HBM), vmem, vmem],
        out_specs=[vmem] * 4,
        out_shape=[
            jax.ShapeDtypeStruct((count, rank), jnp.float32),
            part,
            part,
            jax.ShapeDtypeStruct((rank, rank), jnp.float32),
        ],
        scratch_shapes=[
            pltpu.VMEM((count, depth, width), jnp.float32),
            pltpu.VMEM((rank, rank), jnp.float32),
            pltpu.VMEM((count, rank, width), jnp.float32),
            pltpu.VMEM((rank, width), jnp.float32),
            pltpu.VMEM((2 * rank, depth), jnp.bfloat16),
            pltpu.VMEM((rank, 128), jnp.float32),
            pltpu.VMEM((rank, 128), jnp.float32),
            pltpu.SemaphoreType.DMA((count,)),
        ],
        compiler_params=pltpu.CompilerParams(vmem_limit_bytes=LIMIT),
        cost_estimate=pl.CostEstimate(
            flops=6 * count * depth * width * rank, bytes_accessed=turned.size * 4, transcendentals=0
        ),
    )(turned, factor_b, factor_c)


def scales(gram, count):
    diagonal = jnp.where(eye_mask(gram.shape[0]), gram, 0.0)
    row = jnp.sqrt(count / (jnp.sum(diagonal, axis=0, keepdims=True) + 1e-06))
    column = jnp.sqrt(count / (jnp.sum(diagonal, axis=1, keepdims=True) + 1e-06))
    return row, column


def second_kernel(count, all_ref, own_ref, gram_c_ref, new_ref, gram_ref, inv_ref, work):
    rows = all_ref[...]
    raw = dot(rows.T, rows)
    row, column = scales(raw, count)
    gram = raw * row * column
    gram_ref[...] = gram
    new_ref[...] = own_ref[...] * row
    matrix, mean = system(gram, gram_c_ref[...])
    work[...] = matrix
    invert(work)
    inv_ref[...] = work[...] * (column * (1.0 / mean))


def second_call(gathered, own, gram_c):
    rank = own.shape[1]
    square = jax.ShapeDtypeStruct((rank, rank), jnp.float32)
    return pl.pallas_call(
        functools.partial(second_kernel, float(gathered.shape[0])),
        out_shape=[jax.ShapeDtypeStruct(own.shape, jnp.float32), square, square],
        scratch_shapes=[pltpu.VMEM((rank, rank), jnp.float32)],
        compiler_params=pltpu.CompilerParams(vmem_limit_bytes=SMALL),
        cost_estimate=pl.CostEstimate(flops=10**10, bytes_accessed=10**6, transcendentals=0),
    )(gathered, own, gram_c)


def third_kernel(
    x_hbm, a_ref, own_ref, other_ref, inv_ref, raw_ref, gram_ref, keep_ref, send_ref, x_ref, halves, total, sems
):
    copies = fetch(x_hbm, x_ref, sems)
    count, depth, width = x_ref.shape
    half = own_ref.shape[0]
    core = lax.axis_index("gx") & 1
    mine = inv_ref[pl.ds(pl.multiple_of(core * half, half), half), :]
    others = inv_ref[pl.ds(pl.multiple_of((1 - core) * half, half), half), :]
    raw = mul3(own_ref[...].T, mine) + mul3(other_ref[...].T, others)
    high, low = split(raw)
    halves[0] = high
    halves[1] = low
    turned = raw.T
    turned_high, turned_low = split(turned)
    gram = mul(turned_high, high) + (mul(turned_low, high) + mul(turned_high, low))
    row, column = scales(gram, float(width))
    raw_ref[...] = raw * row
    gram_ref[...] = gram * row * column
    for copy in copies:
        copy.wait()
    for i in range(count):
        scale = a_ref[i : i + 1, :] * row
        for at, size in chunks(depth, 192):
            high, low = split(x_ref[i, at : at + size, :])
            block = mul(high, halves[0])
            block = block + mul(low, halves[0])
            block = block + mul(high, halves[1])
            block = block * scale
            if i:
                block = block + total[at : at + size, :]
            total[at : at + size, :] = block
    members, padded, _ = keep_ref.shape
    rows = depth // (2 * members)
    bits = members.bit_length() - 1
    for place in range(members):
        chip = sum(((place >> b) & 1) << (bits - 1 - b) for b in range(bits))
        one = total[2 * chip * rows : (2 * chip + 1) * rows, :]
        two = total[(2 * chip + 1) * rows : (2 * chip + 2) * rows, :]
        keep_ref[place, :rows, :] = jnp.where(core == 0, one, two)
        send_ref[place, :rows, :] = jnp.where(core == 0, two, one)
        if padded > rows:
            rest = jnp.zeros((padded - rows, raw.shape[1]), jnp.float32)
            keep_ref[place, rows:, :] = rest
            send_ref[place, rows:, :] = rest


def third_call(turned, new_a, own, other, inv, devices):
    count, depth, width = turned.shape
    rank = new_a.shape[1]
    padded = -(-(depth // devices) // 8) * 8
    vmem = pl.BlockSpec(memory_space=pltpu.VMEM)
    part = jax.ShapeDtypeStruct((devices // 2, padded, rank), jnp.float32)
    return pl.pallas_call(
        third_kernel,
        in_specs=[pl.BlockSpec(memory_space=pltpu.HBM)] + [vmem] * 4,
        out_specs=[vmem] * 4,
        out_shape=[
            jax.ShapeDtypeStruct((width, rank), jnp.float32),
            jax.ShapeDtypeStruct((rank, rank), jnp.float32),
            part,
            part,
        ],
        scratch_shapes=[
            pltpu.VMEM((count, depth, width), jnp.float32),
            pltpu.VMEM((2, width, rank), jnp.bfloat16),
            pltpu.VMEM((depth, rank), jnp.float32),
            pltpu.SemaphoreType.DMA((count,)),
        ],
        compiler_params=pltpu.CompilerParams(vmem_limit_bytes=LIMIT),
        cost_estimate=pl.CostEstimate(
            flops=6 * count * depth * width * rank, bytes_accessed=turned.size * 4, transcendentals=0
        ),
    )(turned, new_a, own, other, inv)


def fourth_kernel(a_ref, b_ref, out_ref):
    matrix, mean = system(a_ref[...], b_ref[...])
    out_ref[...] = matrix
    invert(out_ref)
    out_ref[...] = out_ref[...] * (1.0 / mean)


def fourth_call(gram_a, gram_b):
    return pl.pallas_call(
        fourth_kernel,
        out_shape=jax.ShapeDtypeStruct(gram_a.shape, jnp.float32),
        compiler_params=pltpu.CompilerParams(vmem_limit_bytes=SMALL),
        cost_estimate=pl.CostEstimate(flops=10**10, bytes_accessed=10**6, transcendentals=0),
    )(gram_a, gram_b)


def swap(x, bit):
    devices = lax.axis_size("gx")
    return lax.ppermute(x, "gx", [(i, i ^ (1 << bit)) for i in range(devices)])


def exchange(x, groups):
    return lax.all_to_all(x, "gx", 0, 0, axis_index_groups=groups, tiled=True)


def chips():
    members = lax.axis_size("gx") // 2
    bits = members.bit_length() - 1
    order = [sum(((p >> b) & 1) << (bits - 1 - b) for b in range(bits)) for p in range(members)]
    return [[2 * chip + core for chip in order] for core in range(2)]


def scatter(keep, send):
    return exchange(keep + swap(send, 0), chips())


def halve(keep, send, width):
    me = lax.axis_index("gx")
    x = keep + swap(send, 0)
    tails = x[:1, :, width:]
    x = x[:, :, :width]
    steps = x.shape[0].bit_length() - 1
    for bit in range(1, steps + 1):
        mine = (me >> bit) & 1
        half, count = x.shape[0] // 2, tails.shape[0]
        x = x.reshape((2, half) + x.shape[1:])
        keep = lax.dynamic_index_in_dim(x, mine, 0, keepdims=False)
        send = lax.dynamic_index_in_dim(x, 1 - mine, 0, keepdims=False)
        rows, extra = tails.shape[1:]
        if count <= half:
            riders = jnp.pad(tails, ((0, half - count), (0, 0), (0, 0)))
        else:
            riders = tails.reshape(half, count // half, rows, extra).transpose(0, 2, 1, 3)
            riders = riders.reshape(half, rows, count // half * extra)
        got = swap(jnp.concatenate([send, riders], axis=2), bit)
        x = keep + got[:, :, :width]
        riders = got[:, :, width:]
        if count <= half:
            riders = riders[:count]
        else:
            riders = riders.reshape(half, rows, count // half, extra).transpose(0, 2, 1, 3)
            riders = riders.reshape(count, rows, extra)
        tails = jnp.concatenate([tails, riders], axis=0)
    return x[0], tails


def spread_out(x):
    members = lax.axis_size("gx") // 2
    return exchange(jnp.broadcast_to(x[None], (members,) + x.shape), chips())


def unpack(tail, count, rank):
    members, rows, extra = tail.shape
    tail = tail.reshape(members, rows, extra // 128, 128).transpose(0, 2, 1, 3)
    tail = tail.reshape(members, 2, rank // 128, count, 128).transpose(0, 1, 3, 2, 4)
    return tail.reshape(members * 2 * count, rank)


def gather_small(x):
    devices = lax.axis_size("gx")
    x = exchange(jnp.broadcast_to(x[None], (devices,) + x.shape), None)
    return x.reshape((-1,) + x.shape[2:])


def local(tensor, factor_b, factor_c):
    devices = lax.axis_size("gx")
    me = lax.axis_index("gx")
    count, total_second, total_third = tensor.shape
    turned = jnp.swapaxes(tensor, 1, 2)
    raw_a, keep, send, gram_c = first_call(turned, factor_b, factor_c, devices)
    rank = raw_a.shape[1]
    side_b, tails = halve(keep, send, total_second)
    gathered = unpack(tails, count, rank)
    new_a, gram_a, inv_b = second_call(gathered, raw_a, gram_c)
    own = spread_out(side_b)
    own, inv_b = lax.optimization_barrier((own, inv_b))
    other = swap(own, 0)
    whole = (rank // 2, total_second)
    all_b, gram_b, keep, send = third_call(
        turned, new_a, own.reshape(whole), other.reshape(whole), inv_b, devices
    )
    rows_b = total_second // devices
    new_b = lax.dynamic_slice_in_dim(all_b, me * rows_b, rows_b, axis=0)
    inv_c = fourth_call(gram_a, gram_b)
    side_c = jnp.sum(scatter(keep, send), axis=0)
    raw_c = dot(side_c, inv_c)[: total_third // devices]
    sums = jnp.sum(gather_small(jnp.sum(raw_c * raw_c, axis=0, keepdims=True)), axis=0)
    new_c = raw_c * jnp.sqrt(total_third / (sums + 1e-06))
    return (new_a, new_b, new_c)


def solution(mesh):
    placed = (P(("grp", "gx"), None, None), P("grp", None), P("grp", None))
    return jax.shard_map(
        local,
        mesh=mesh,
        in_specs=placed,
        out_specs=(P(("grp", "gx"), None), P(("grp", "gx"), None), P(("grp", "gx"), None)),
        check_vma=False,
    )
```

profile of v0, /device:TPU:0, one launch (start us, length us, event | category | flops | bytes accessed | tf_op | source)
XLA Modules:
  0.0 105.7 jit_solution(5388136526027243755)
XLA Ops:
  0.6 1.3 %copy-done = f32[1152,256]{1,0:T(8,128)S(1)} copy-done((f32[1152,256]{1,0:T(8,128)S(1)}, f32[1152,256]{1,0:T(8,128)}, u32[]{:S(2)}) %copy-start) | copy-done | bytes 1179672
  1.9 1.1 %copy-done.1 = f32[576,256]{1,0:T(8,128)S(1)} copy-done((f32[576,256]{1,0:T(8,128)S(1)}, f32[576,256]{1,0:T(8,128)}, u32[]{:S(2)}) %copy-start.1) | copy-done | bytes 589848
  3.0 15.0 %shard_map.58 = (f32[4,256]{1,0:T(4,128)S(1)}, f32[8,16,1280]{2,1,0:T(8,128)S(1)}, f32[8,16,1280]{2,1,0:T(8,128)S(1)}, f32[256,256]{1,0:T(8,128)S(1)}) custom-call(f32[4,576,1152]{2,1,0:T(8,128)} %bitcast.45, f32[1152,256]{1,0:T(8,128)S(1)} %copy-done, f32[576,256]{1,0:T(8,128)S(1)} %copy-done.1), custom_call_target="tpu_custom_call" | custom-call | flops 4076863488 | bytes 10616832 | tf_op jit(solution)/shard_map/pallas_call | solution.py:261
  18.0 0.5 collective-permute-start
  18.6 1.7 %collective-permute-done = f32[8,16,1280]{2,1,0:T(8,128)S(1)} collective-permute-done((f32[8,16,1280]{2,1,0:T(8,128)S(1)}, f32[8,16,1280]{2,1,0:T(8,128)S(1)}, u32[]{:S(2)}, u32[]{:S(2)}) %collective-permute-start) | collective-permute-done | bytes 655392 | tf_op jit(solution)/shard_map/ppermute | solution.py:414
  20.3 0.1 add.54
  20.5 2.9 %collective-permute-start.1 = (f32[4,16,1280]{2,1,0:T(8,128)S(1)}, f32[4,16,1280]{2,1,0:T(8,128)S(1)}, u32[]{:S(2)}, u32[]{:S(2)}) collective-permute-start(f32[4,16,1280]{2,1,0:T(8,128)S(1)} %select_maximum_fusion), channel_id=1, source_target_pairs={{0,2},{1,3},{2,0},{3,1},{4,6},{5,7},{6,4},{7,5},{8,10},{9,11},{10,... | collective-permute-start | bytes 983048 | tf_op jit(solution)/shard_map/ppermute | solution.py:414
  23.4 8.0 %collective-permute-done.1 = f32[4,16,1280]{2,1,0:T(8,128)S(1)} collective-permute-done((f32[4,16,1280]{2,1,0:T(8,128)S(1)}, f32[4,16,1280]{2,1,0:T(8,128)S(1)}, u32[]{:S(2)}, u32[]{:S(2)}) %collective-permute-start.1) | collective-permute-done | bytes 327712 | tf_op jit(solution)/shard_map/ppermute | solution.py:414
  31.5 1.9 %collective-permute-start.2 = (f32[2,16,1280]{2,1,0:T(8,128)S(1)}, f32[2,16,1280]{2,1,0:T(8,128)S(1)}, u32[]{:S(2)}, u32[]{:S(2)}) collective-permute-start(f32[2,16,1280]{2,1,0:T(8,128)S(1)} %maximum_maximum_fusion), channel_id=1, source_target_pairs={{0,4},{1,5},{2,6},{3,7},{4,0},{5,1},{6,2},{7,3},{8,12},{9,13},{10,... | collective-permute-start | bytes 491528 | tf_op jit(solution)/shard_map/ppermute | solution.py:414
  33.4 3.9 %collective-permute-done.2 = f32[2,16,1280]{2,1,0:T(8,128)S(1)} collective-permute-done((f32[2,16,1280]{2,1,0:T(8,128)S(1)}, f32[2,16,1280]{2,1,0:T(8,128)S(1)}, u32[]{:S(2)}, u32[]{:S(2)}) %collective-permute-start.2) | collective-permute-done | bytes 163872 | tf_op jit(solution)/shard_map/ppermute | solution.py:414
  37.5 2.6 %collective-permute-start.3 = (f32[1,16,1664]{2,1,0:T(8,128)S(1)}, f32[1,16,1664]{2,1,0:T(8,128)S(1)}, u32[]{:S(2)}, u32[]{:S(2)}) collective-permute-start(f32[1,16,1664]{2,1,0:T(8,128)S(1)} %pad_maximum_fusion), channel_id=1, source_target_pairs={{0,8},{1,9},{2,10},{3,11},{4,12},{5,13},{6,14},{7,15},{8,0},{9,1},... | collective-permute-start | bytes 319496 | tf_op jit(solution)/shard_map/ppermute | solution.py:414
  40.0 4.3 %collective-permute-done.3 = f32[1,16,1664]{2,1,0:T(8,128)S(1)} collective-permute-done((f32[1,16,1664]{2,1,0:T(8,128)S(1)}, f32[1,16,1664]{2,1,0:T(8,128)S(1)}, u32[]{:S(2)}, u32[]{:S(2)}) %collective-permute-start.3) | collective-permute-done | bytes 106528 | tf_op jit(solution)/shard_map/ppermute | solution.py:414
  44.3 0.8 broadcast_in_dim.14
  45.2 5.6 %all-to-all-start = ((f32[8,16,1152]{2,1,0:T(8,128)}), f32[8,16,1152]{2,1,0:T(8,128)S(1)}, u32[]{:S(2)}, u32[]{:S(2)}) async-start(f32[8,16,1152]{2,1,0:T(8,128)} %broadcast_in_dim.14), calls=%async_computation | async-start | bytes 1179648 | tf_op jit(solution)/shard_map/all_to_all | solution.py:418
  50.9 9.6 %shard_map.59 = (f32[4,256]{1,0:T(4,128)}, f32[256,256]{1,0:T(8,128)S(1)}, f32[256,256]{1,0:T(8,128)S(1)}) custom-call(f32[64,256]{1,0:T(8,128)S(1)} %bitcast.33, f32[4,256]{1,0:T(4,128)S(1)} %get-tuple-element.18.own_ref, f32[256,256]{1,0:T(8,128)S(1)} %get-tuple-element.19.gram_c_ref), custom_call_target="tpu_custom_call" | custom-call | flops 10000000000 | bytes 1000000 | tf_op jit(solution)/shard_map/pallas_call | solution.py:311
  60.4 2.9 %all-to-all-done = f32[8,16,1152]{2,1,0:T(8,128)S(1)} async-done(((f32[8,16,1152]{2,1,0:T(8,128)}), f32[8,16,1152]{2,1,0:T(8,128)S(1)}, u32[]{:S(2)}, u32[]{:S(2)}) %all-to-all-start) | async-done | bytes 589856 | tf_op jit(solution)/shard_map/all_to_all | solution.py:418
  63.4 0.0 collective-permute-start.4
  63.4 2.0 %collective-permute-done.4 = f32[8,16,1152]{2,1,0:T(8,128)S(1)} collective-permute-done((f32[8,16,1152]{2,1,0:T(8,128)S(1)}, f32[8,16,1152]{2,1,0:T(8,128)S(1)}, u32[]{:S(2)}, u32[]{:S(2)}) %collective-permute-start.4) | collective-permute-done | bytes 589856 | tf_op jit(solution)/shard_map/ppermute | solution.py:414
  65.4 0.7 copy-done.2
  66.1 9.9 %shard_map.60 = (f32[1152,256]{1,0:T(8,128)S(1)}, f32[256,256]{1,0:T(8,128)S(1)}, f32[8,40,256]{2,1,0:T(8,128)S(1)}, f32[8,40,256]{2,1,0:T(8,128)S(1)}) custom-call(f32[4,576,1152]{2,1,0:T(8,128)} %bitcast.46, f32[4,256]{1,0:T(4,128)S(1)} %copy-done.2, f32[128,1152]{1,0:T(8,128)S(1)} %bitcast.32, f32[128,1152]{1,0:T(8,128)S(1)} %bitcast.34, ...), custom_call_target="tpu_custom_call" | custom-call | flops 4076863488 | bytes 10616832 | tf_op jit(solution)/shard_map/pallas_call | solution.py:373
  76.0 0.2 collective-permute-start.5
  76.2 1.5 %collective-permute-done.5 = f32[8,40,256]{2,1,0:T(8,128)S(1)} collective-permute-done((f32[8,40,256]{2,1,0:T(8,128)S(1)}, f32[8,40,256]{2,1,0:T(8,128)S(1)}, u32[]{:S(2)}, u32[]{:S(2)}) %collective-permute-start.5) | collective-permute-done | bytes 327712 | tf_op jit(solution)/shard_map/ppermute | solution.py:414
  77.7 0.8 add.65
  78.5 4.4 %all-to-all-start.1 = ((f32[8,40,256]{2,1,0:T(8,128)}), f32[8,40,256]{2,1,0:T(8,128)S(1)}, u32[]{:S(2)}, u32[]{:S(2)}) async-start(f32[8,40,256]{2,1,0:T(8,128)} %add.65), calls=%async_computation.1 | async-start | bytes 655360 | tf_op jit(solution)/shard_map/all_to_all | solution.py:418
  82.8 8.6 %shard_map.61 = f32[256,256]{1,0:T(8,128)S(1)} custom-call(f32[256,256]{1,0:T(8,128)S(1)} %get-tuple-element.27.a_ref, f32[256,256]{1,0:T(8,128)S(1)} %get-tuple-element.28.b_ref), custom_call_target="tpu_custom_call" | custom-call | flops 10000000000 | bytes 1000000 | tf_op jit(solution)/shard_map/pallas_call | solution.py:404
  91.5 2.0 %all-to-all-done.1 = f32[8,40,256]{2,1,0:T(8,128)S(1)} async-done(((f32[8,40,256]{2,1,0:T(8,128)}), f32[8,40,256]{2,1,0:T(8,128)S(1)}, u32[]{:S(2)}, u32[]{:S(2)}) %all-to-all-start.1) | async-done | bytes 327712 | tf_op jit(solution)/shard_map/all_to_all | solution.py:418
  93.5 0.3 multiply_reduce_fusion
  93.7 0.6 broadcast_in_dim.15
  94.4 4.1 %all-to-all-start.2 = ((f32[16,1,256]{2,1,0:T(1,128)}), f32[16,1,256]{2,1,0:T(1,128)S(1)}, u32[]{:S(2)}, u32[]{:S(2)}) async-start(f32[16,1,256]{2,1,0:T(1,128)} %broadcast_in_dim.15), calls=%async_computation.2 | async-start | bytes 32768 | tf_op jit(solution)/shard_map/all_to_all | solution.py:418
  98.5 0.6 constant_dynamic-slice_fusion
  99.2 5.8 %all-to-all-done.2 = f32[16,1,256]{2,1,0:T(1,128)S(1)} async-done(((f32[16,1,256]{2,1,0:T(1,128)}), f32[16,1,256]{2,1,0:T(1,128)S(1)}, u32[]{:S(2)}, u32[]{:S(2)}) %all-to-all-start.2) | async-done | bytes 16416 | tf_op jit(solution)/shard_map/all_to_all | solution.py:418
  105.1 0.6 broadcast_multiply_fusion
  (27 shorter events, 0.4 us)
Async XLA Ops:
  0.6 1.3 %copy-start = (f32[1152,256]{1,0:T(8,128)S(1)}, f32[1152,256]{1,0:T(8,128)}, u32[]{:S(2)}) copy-start(f32[1152,256]{1,0:T(8,128)} %b_ref.1) | copy-start | bytes 3538948
  1.9 1.1 %copy-start.1 = (f32[576,256]{1,0:T(8,128)S(1)}, f32[576,256]{1,0:T(8,128)}, u32[]{:S(2)}) copy-start(f32[576,256]{1,0:T(8,128)} %c_ref.1) | copy-start | bytes 1769476
  18.0 2.3 %collective-permute-start = (f32[8,16,1280]{2,1,0:T(8,128)S(1)}, f32[8,16,1280]{2,1,0:T(8,128)S(1)}, u32[]{:S(2)}, u32[]{:S(2)}) collective-permute-start(f32[8,16,1280]{2,1,0:T(8,128)S(1)} %get-tuple-element.17), channel_id=1, source_target_pairs={{0,1},{1,0},{2,3},{3,2},{4,5},{5,4},{6,7},{7,6},{8,9},{9,8},{10,11... | collective-permute-start | bytes 1966088 | tf_op jit(solution)/shard_map/ppermute | solution.py:414
  20.5 10.9 %collective-permute-start.1 = (f32[4,16,1280]{2,1,0:T(8,128)S(1)}, f32[4,16,1280]{2,1,0:T(8,128)S(1)}, u32[]{:S(2)}, u32[]{:S(2)}) collective-permute-start(f32[4,16,1280]{2,1,0:T(8,128)S(1)} %select_maximum_fusion), channel_id=1, source_target_pairs={{0,2},{1,3},{2,0},{3,1},{4,6},{5,7},{6,4},{7,5},{8,10},{9,11},{10,... | collective-permute-start | bytes 983048 | tf_op jit(solution)/shard_map/ppermute | solution.py:414
  31.5 5.8 %collective-permute-start.2 = (f32[2,16,1280]{2,1,0:T(8,128)S(1)}, f32[2,16,1280]{2,1,0:T(8,128)S(1)}, u32[]{:S(2)}, u32[]{:S(2)}) collective-permute-start(f32[2,16,1280]{2,1,0:T(8,128)S(1)} %maximum_maximum_fusion), channel_id=1, source_target_pairs={{0,4},{1,5},{2,6},{3,7},{4,0},{5,1},{6,2},{7,3},{8,12},{9,13},{10,... | collective-permute-start | bytes 491528 | tf_op jit(solution)/shard_map/ppermute | solution.py:414
  37.5 6.8 %collective-permute-start.3 = (f32[1,16,1664]{2,1,0:T(8,128)S(1)}, f32[1,16,1664]{2,1,0:T(8,128)S(1)}, u32[]{:S(2)}, u32[]{:S(2)}) collective-permute-start(f32[1,16,1664]{2,1,0:T(8,128)S(1)} %pad_maximum_fusion), channel_id=1, source_target_pairs={{0,8},{1,9},{2,10},{3,11},{4,12},{5,13},{6,14},{7,15},{8,0},{9,1},... | collective-permute-start | bytes 319496 | tf_op jit(solution)/shard_map/ppermute | solution.py:414
  45.2 18.2 %all-to-all-start = ((f32[8,16,1152]{2,1,0:T(8,128)}), f32[8,16,1152]{2,1,0:T(8,128)S(1)}, u32[]{:S(2)}, u32[]{:S(2)}) async-start(f32[8,16,1152]{2,1,0:T(8,128)} %broadcast_in_dim.14), calls=%async_computation | async-start | bytes 1179648 | tf_op jit(solution)/shard_map/all_to_all | solution.py:418
  63.4 2.0 %collective-permute-start.4 = (f32[8,16,1152]{2,1,0:T(8,128)S(1)}, f32[8,16,1152]{2,1,0:T(8,128)S(1)}, u32[]{:S(2)}, u32[]{:S(2)}) collective-permute-start(f32[8,16,1152]{2,1,0:T(8,128)S(1)} %all-to-all-done), channel_id=1, source_target_pairs={{0,1},{1,0},{2,3},{3,2},{4,5},{5,4},{6,7},{7,6},{8,9},{9,8},{10,11... | collective-permute-start | bytes 1769480 | tf_op jit(solution)/shard_map/ppermute | solution.py:414
  65.4 0.7 copy-start.2
  76.0 1.7 %collective-permute-start.5 = (f32[8,40,256]{2,1,0:T(8,128)S(1)}, f32[8,40,256]{2,1,0:T(8,128)S(1)}, u32[]{:S(2)}, u32[]{:S(2)}) collective-permute-start(f32[8,40,256]{2,1,0:T(8,128)S(1)} %get-tuple-element.26), channel_id=1, source_target_pairs={{0,1},{1,0},{2,3},{3,2},{4,5},{5,4},{6,7},{7,6},{8,9},{9,8},{10,11... | collective-permute-start | bytes 983048 | tf_op jit(solution)/shard_map/ppermute | solution.py:414
  78.5 15.0 %all-to-all-start.1 = ((f32[8,40,256]{2,1,0:T(8,128)}), f32[8,40,256]{2,1,0:T(8,128)S(1)}, u32[]{:S(2)}, u32[]{:S(2)}) async-start(f32[8,40,256]{2,1,0:T(8,128)} %add.65), calls=%async_computation.1 | async-start | bytes 655360 | tf_op jit(solution)/shard_map/all_to_all | solution.py:418
  94.4 10.6 %all-to-all-start.2 = ((f32[16,1,256]{2,1,0:T(1,128)}), f32[16,1,256]{2,1,0:T(1,128)S(1)}, u32[]{:S(2)}, u32[]{:S(2)}) async-start(f32[16,1,256]{2,1,0:T(1,128)} %broadcast_in_dim.15), calls=%async_computation.2 | async-start | bytes 32768 | tf_op jit(solution)/shard_map/all_to_all | solution.py:418
where the time goes:
time: 106 us
  Pallas kernels  43.2 us (41%)
  waiting for transfers between devices  32.2 us (30%)
  starting transfers between devices  22.2 us (21%)
  local copies, waits for them, and re-layouts  5.3 us (5%)
  other arithmetic  1.72 us (2%)
    ppermute x6, waiting for transfers between devices, swap(): return lax.ppermute(x, 'gx', [(i, i ^ 1 << bit) for i in range(devices)])  21.5 us
    pallas_call x1, Pallas kernels, first_call(): pl.pallas_call(first_kernel, in_specs=[pl.BlockSpec(memory_space=pltpu.HB...  15 us
    all_to_all x3, starting transfers between devices, exchange(): return lax.all_to_all(x, 'gx', 0, 0, axis_index_groups=groups, tiled=True)  14.1 us
    all_to_all x3, waiting for transfers between devices, exchange(): return lax.all_to_all(x, 'gx', 0, 0, axis_index_groups=groups, tiled=True)  10.8 us
    pallas_call x1, Pallas kernels, third_call(): pl.pallas_call(third_kernel, in_specs=[pl.BlockSpec(memory_space=pltpu.HB...  9.94 us
    pallas_call x1, Pallas kernels, second_call(): pl.pallas_call(functools.partial(second_kernel, float(gathered.shape[0]))...  9.56 us
    pallas_call x1, Pallas kernels, fourth_call(): pl.pallas_call(fourth_kernel, out_shape=jax.ShapeDtypeStruct(gram_a.shape...  8.65 us
    ppermute x6, starting transfers between devices, swap(): return lax.ppermute(x, 'gx', [(i, i ^ 1 << bit) for i in range(devices)])  8.1 us
  transfers between devices with their start and end apart: 9, of which 9 were waited for; matrix products, arithmetic and copies ran while one was open for 1% of the time, Pallas kernels for 17%

commit v1 on v0

--- a/solution.py
+++ b/solution.py
@@ -10,7 +10,7 @@
 HIGH = lax.Precision.HIGHEST
 PANEL = 32
 LIMIT = 50 * 1024 * 1024
-SMALL = 8 * 1024 * 1024
+SMALL = 12 * 1024 * 1024
 
 
 def dot(a, b):
@@ -212,16 +212,18 @@
     gram_c = mul3(c_turned, c)
     gram_ref[...] = gram_c
     turned[...] = b_ref[...].T
+    sums[...] = jnp.zeros_like(sums)
+    copies[0].wait()
+    contraction = contract(x_ref, stack, turned, out, sums, partial)
+    units = len(chunks(width, 256))
+    for _ in range(units):
+        next(contraction)
     matrix, mean = system(mul3(turned[...], b_ref[...]), gram_c)
     inv[...] = matrix
-    sums[...] = jnp.zeros_like(sums)
-    for copy in copies:
+    for copy in copies[1:]:
         copy.wait()
     weave(
-        eliminate(inv),
-        contract(x_ref, stack, turned, out, sums, partial),
-        (rank // PANEL) * (PANEL // 2 + 1),
-        count * len(chunks(width, 256)),
+        eliminate(inv), contraction, (rank // PANEL) * (PANEL // 2 + 1), (count - 1) * units
     )
     raw = dot(inv[...], sums[...]) * (1.0 / mean)
     raw_rows = raw.T[:count, :]
@@ -292,13 +294,14 @@
     return row, column
 
 
-def second_kernel(count, all_ref, own_ref, gram_c_ref, new_ref, gram_ref, inv_ref, work):
+def second_kernel(count, all_ref, own_ref, gram_c_ref, new_ref, row_ref, gram_ref, inv_ref, work):
     rows = all_ref[...]
     raw = dot(rows.T, rows)
     row, column = scales(raw, count)
     gram = raw * row * column
     gram_ref[...] = gram
     new_ref[...] = own_ref[...] * row
+    row_ref[...] = row
     matrix, mean = system(gram, gram_c_ref[...])
     work[...] = matrix
     invert(work)
@@ -310,7 +313,12 @@
     square = jax.ShapeDtypeStruct((rank, rank), jnp.float32)
     return pl.pallas_call(
         functools.partial(second_kernel, float(gathered.shape[0])),
-        out_shape=[jax.ShapeDtypeStruct(own.shape, jnp.float32), square, square],
+        out_shape=[
+            jax.ShapeDtypeStruct(own.shape, jnp.float32),
+            jax.ShapeDtypeStruct((1, rank), jnp.float32),
+            square,
+            square,
+        ],
         scratch_shapes=[pltpu.VMEM((rank, rank), jnp.float32)],
         compiler_params=pltpu.CompilerParams(vmem_limit_bytes=SMALL),
         cost_estimate=pl.CostEstimate(flops=10**10, bytes_accessed=10**6, transcendentals=0),
@@ -318,7 +326,7 @@
 
 
 def third_kernel(
-    x_hbm, a_ref, own_ref, other_ref, inv_ref, raw_ref, gram_ref, keep_ref, send_ref, x_ref, halves, total, sems
+    x_hbm, a_ref, scale_ref, own_ref, other_ref, inv_ref, raw_ref, keep_ref, send_ref, x_ref, halves, total, sems
 ):
     copies = fetch(x_hbm, x_ref, sems)
     count, depth, width = x_ref.shape
@@ -327,19 +335,14 @@
     mine = inv_ref[pl.ds(pl.multiple_of(core * half, half), half), :]
     others = inv_ref[pl.ds(pl.multiple_of((1 - core) * half, half), half), :]
     raw = mul3(own_ref[...].T, mine) + mul3(other_ref[...].T, others)
-    high, low = split(raw)
-    halves[0] = high
-    halves[1] = low
-    turned = raw.T
-    turned_high, turned_low = split(turned)
-    gram = mul(turned_high, high) + (mul(turned_low, high) + mul(turned_high, low))
-    row, column = scales(gram, float(width))
+    halves[0], halves[1] = split(raw)
+    row = jnp.sqrt(float(width) / (jnp.sum(raw * raw, axis=0, keepdims=True) + 1e-06))
     raw_ref[...] = raw * row
-    gram_ref[...] = gram * row * column
+    both = scale_ref[...] * row
     for copy in copies:
         copy.wait()
     for i in range(count):
-        scale = a_ref[i : i + 1, :] * row
+        scale = a_ref[i : i + 1, :] * both
         for at, size in chunks(depth, 192):
             high, low = split(x_ref[i, at : at + size, :])
             block = mul(high, halves[0])
@@ -364,22 +367,17 @@
             send_ref[place, rows:, :] = rest
 
 
-def third_call(turned, new_a, own, other, inv, devices):
+def third_call(turned, raw_a, scale_a, own, other, inv, devices):
     count, depth, width = turned.shape
-    rank = new_a.shape[1]
+    rank = raw_a.shape[1]
     padded = -(-(depth // devices) // 8) * 8
     vmem = pl.BlockSpec(memory_space=pltpu.VMEM)
     part = jax.ShapeDtypeStruct((devices // 2, padded, rank), jnp.float32)
     return pl.pallas_call(
         third_kernel,
-        in_specs=[pl.BlockSpec(memory_space=pltpu.HBM)] + [vmem] * 4,
-        out_specs=[vmem] * 4,
-        out_shape=[
-            jax.ShapeDtypeStruct((width, rank), jnp.float32),
-            jax.ShapeDtypeStruct((rank, rank), jnp.float32),
-            part,
-            part,
-        ],
+        in_specs=[pl.BlockSpec(memory_space=pltpu.HBM)] + [vmem] * 5,
+        out_specs=[vmem] * 3,
+        out_shape=[jax.ShapeDtypeStruct((width, rank), jnp.float32), part, part],
         scratch_shapes=[
             pltpu.VMEM((count, depth, width), jnp.float32),
             pltpu.VMEM((2, width, rank), jnp.bfloat16),
@@ -390,23 +388,24 @@
         cost_estimate=pl.CostEstimate(
             flops=6 * count * depth * width * rank, bytes_accessed=turned.size * 4, transcendentals=0
         ),
-    )(turned, new_a, own, other, inv)
+    )(turned, raw_a, scale_a, own, other, inv)
 
 
 def fourth_kernel(a_ref, b_ref, out_ref):
-    matrix, mean = system(a_ref[...], b_ref[...])
+    b = b_ref[...]
+    matrix, mean = system(a_ref[...], mul3(b.T, b))
     out_ref[...] = matrix
     invert(out_ref)
     out_ref[...] = out_ref[...] * (1.0 / mean)
 
 
-def fourth_call(gram_a, gram_b):
+def fourth_call(gram_a, all_b):
     return pl.pallas_call(
         fourth_kernel,
         out_shape=jax.ShapeDtypeStruct(gram_a.shape, jnp.float32),
         compiler_params=pltpu.CompilerParams(vmem_limit_bytes=SMALL),
         cost_estimate=pl.CostEstimate(flops=10**10, bytes_accessed=10**6, transcendentals=0),
-    )(gram_a, gram_b)
+    )(gram_a, all_b)
 
 
 def swap(x, bit):
@@ -425,6 +424,15 @@
     return [[2 * chip + core for chip in order] for core in range(2)]
 
 
+def quads():
+    devices = lax.axis_size("gx")
+    return [
+        [8 * group + core + place for place in (0, 4, 2, 6)]
+        for core in range(2)
+        for group in range(devices // 8)
+    ]
+
+
 def scatter(keep, send):
     return exchange(keep + swap(send, 0), chips())
 
@@ -432,10 +440,11 @@
 def halve(keep, send, width):
     me = lax.axis_index("gx")
     x = keep + swap(send, 0)
-    tails = x[:1, :, width:]
-    x = x[:, :, :width]
+    x = exchange(x, quads()).reshape((4, x.shape[0] // 4) + x.shape[1:])
+    tails = x[:, 0, :, width:]
+    x = jnp.sum(x[:, :, :, :width], axis=0)
     steps = x.shape[0].bit_length() - 1
-    for bit in range(1, steps + 1):
+    for bit in range(3, steps + 3):
         mine = (me >> bit) & 1
         half, count = x.shape[0] // 2, tails.shape[0]
         x = x.reshape((2, half) + x.shape[1:])
@@ -486,17 +495,17 @@
     rank = raw_a.shape[1]
     side_b, tails = halve(keep, send, total_second)
     gathered = unpack(tails, count, rank)
-    new_a, gram_a, inv_b = second_call(gathered, raw_a, gram_c)
+    new_a, scale_a, gram_a, inv_b = second_call(gathered, raw_a, gram_c)
     own = spread_out(side_b)
     own, inv_b = lax.optimization_barrier((own, inv_b))
     other = swap(own, 0)
     whole = (rank // 2, total_second)
-    all_b, gram_b, keep, send = third_call(
-        turned, new_a, own.reshape(whole), other.reshape(whole), inv_b, devices
+    all_b, keep, send = third_call(
+        turned, raw_a, scale_a, own.reshape(whole), other.reshape(whole), inv_b, devices
     )
     rows_b = total_second // devices
     new_b = lax.dynamic_slice_in_dim(all_b, me * rows_b, rows_b, axis=0)
-    inv_c = fourth_call(gram_a, gram_b)
+    inv_c = fourth_call(gram_a, all_b)
     side_c = jnp.sum(scatter(keep, send), axis=0)
     raw_c = dot(side_c, inv_c)[: total_third // devices]
     sums = jnp.sum(gather_small(jnp.sum(raw_c * raw_c, axis=0, keepdims=True)), axis=0)

time: 106 us -> 107 us (level)
  waiting for transfers between devices: 32.2 us -> 30.7 us
  Pallas kernels: 43.2 us -> 44.4 us
    ppermute x6 -> x4, waiting for transfers between devices: 21.5 us -> 9.74 us  [swap(): return lax.ppermute(x, 'gx', [(i, i ^ 1 << bit) for i in range(devices)])]
    all_to_all x3 -> x4, waiting for transfers between devices: 10.8 us -> 20.9 us  [exchange(): return lax.all_to_all(x, 'gx', 0, 0, axis_index_groups=groups, tiled=True)]
    all_to_all x3 -> x4, starting transfers between devices: 14.1 us -> 19.8 us  [exchange(): return lax.all_to_all(x, 'gx', 0, 0, axis_index_groups=groups, tiled=True)]
    ppermute x6 -> x4, starting transfers between devices: 8.1 us -> 3.38 us  [swap(): return lax.ppermute(x, 'gx', [(i, i ^ 1 << bit) for i in range(devices)])]
    unnamed x7 -> x5, local copies, waits for them, and re-layouts: 3.02 us -> 2.33 us
  transfers between devices with their start and end apart: 9 -> 8, of which waited for: 9 -> 8; matrix products, arithmetic and copies ran while one was open for 1% -> 1% of each run, Pallas kernels for 17% -> 18%
where the time goes in v1:
time: 107 us; the launch traced here: 106 us
  Pallas kernels  44.4 us (41%)
  waiting for transfers between devices  30.7 us (29%)
  starting transfers between devices  23.2 us (22%)
  local copies, waits for them, and re-layouts  4.54 us (4%)
  other arithmetic  2.46 us (2%)
    all_to_all x4, waiting for transfers between devices, exchange(): return lax.all_to_all(x, 'gx', 0, 0, axis_index_groups=groups, tiled=True)  20.9 us
    all_to_all x4, starting transfers between devices, exchange(): return lax.all_to_all(x, 'gx', 0, 0, axis_index_groups=groups, tiled=True)  19.8 us
    pallas_call x1, Pallas kernels, first_call(): pl.pallas_call(first_kernel, in_specs=[pl.BlockSpec(memory_space=pltpu.HB...  14.4 us
    pallas_call x1, Pallas kernels, third_call(): pl.pallas_call(third_kernel, in_specs=[pl.BlockSpec(memory_space=pltpu.HB...  10.9 us
    ppermute x4, waiting for transfers between devices, swap(): return lax.ppermute(x, 'gx', [(i, i ^ 1 << bit) for i in range(devices)])  9.74 us
    pallas_call x1, Pallas kernels, fourth_call(): pl.pallas_call(fourth_kernel, out_shape=jax.ShapeDtypeStruct(gram_a.shape...  9.59 us
    pallas_call x1, Pallas kernels, second_call(): pl.pallas_call(functools.partial(second_kernel, float(gathered.shape[0]))...  9.56 us
    ppermute x4, starting transfers between devices, swap(): return lax.ppermute(x, 'gx', [(i, i ^ 1 << bit) for i in range(devices)])  3.38 us
  transfers between devices with their start and end apart: 8, of which 8 were waited for; matrix products, arithmetic and copies ran while one was open for 1% of the time, Pallas kernels for 18%

profile of v1, /device:TPU:0, one launch (start us, length us, event | category | flops | bytes accessed | tf_op | source)
XLA Modules:
  0.0 106.3 jit_solution(9678483644731837179)
XLA Ops:
  0.6 0.0 copy-start
  0.6 1.3 %copy-done = f32[1152,256]{1,0:T(8,128)S(1)} copy-done((f32[1152,256]{1,0:T(8,128)S(1)}, f32[1152,256]{1,0:T(8,128)}, u32[]{:S(2)}) %copy-start) | copy-done | bytes 1179672
  1.9 0.0 copy-start.1
  1.9 1.1 copy-done.1
  3.0 14.4 %shard_map.58 = (f32[4,256]{1,0:T(4,128)S(1)}, f32[8,16,1280]{2,1,0:T(8,128)S(1)}, f32[8,16,1280]{2,1,0:T(8,128)S(1)}, f32[256,256]{1,0:T(8,128)S(1)}) custom-call(f32[4,576,1152]{2,1,0:T(8,128)} %bitcast.33, f32[1152,256]{1,0:T(8,128)S(1)} %copy-done, f32[576,256]{1,0:T(8,128)S(1)} %copy-done.1), custom_call_target="tpu_custom_call" | custom-call | flops 4076863488 | bytes 10616832 | tf_op jit(solution)/shard_map/pallas_call | solution.py:263
  17.4 0.5 collective-permute-start
  17.9 1.7 %collective-permute-done = f32[8,16,1280]{2,1,0:T(8,128)S(1)} collective-permute-done((f32[8,16,1280]{2,1,0:T(8,128)S(1)}, f32[8,16,1280]{2,1,0:T(8,128)S(1)}, u32[]{:S(2)}, u32[]{:S(2)}) %collective-permute-start) | collective-permute-done | bytes 655392 | tf_op jit(solution)/shard_map/ppermute | solution.py:413
  19.6 0.9 add.30
  20.5 5.2 %all-to-all-start = ((f32[8,16,1280]{2,1,0:T(8,128)}), f32[8,16,1280]{2,1,0:T(8,128)S(1)}, u32[]{:S(2)}, u32[]{:S(2)}) async-start(f32[8,16,1280]{2,1,0:T(8,128)} %add.30), calls=%async_computation | async-start | bytes 1310720 | tf_op jit(solution)/shard_map/all_to_all | solution.py:417
  25.7 9.7 %all-to-all-done = f32[8,16,1280]{2,1,0:T(8,128)S(1)} async-done(((f32[8,16,1280]{2,1,0:T(8,128)}), f32[8,16,1280]{2,1,0:T(8,128)S(1)}, u32[]{:S(2)}, u32[]{:S(2)}) %all-to-all-start) | async-done | bytes 655392 | tf_op jit(solution)/shard_map/all_to_all | solution.py:417
  35.5 2.7 %collective-permute-start.1 = (f32[1,16,1664]{2,1,0:T(8,128)S(1)}, f32[1,16,1664]{2,1,0:T(8,128)S(1)}, u32[]{:S(2)}, u32[]{:S(2)}) collective-permute-start(f32[1,16,1664]{2,1,0:T(8,128)S(1)} %pad_maximum_fusion), channel_id=1, source_target_pairs={{0,8},{1,9},{2,10},{3,11},{4,12},{5,13},{6,14},{7,15},{8,0},{9,1},... | collective-permute-start | bytes 319496 | tf_op jit(solution)/shard_map/ppermute | solution.py:413
  38.2 4.5 %collective-permute-done.1 = f32[1,16,1664]{2,1,0:T(8,128)S(1)} collective-permute-done((f32[1,16,1664]{2,1,0:T(8,128)S(1)}, f32[1,16,1664]{2,1,0:T(8,128)S(1)}, u32[]{:S(2)}, u32[]{:S(2)}) %collective-permute-start.1) | collective-permute-done | bytes 106528 | tf_op jit(solution)/shard_map/ppermute | solution.py:413
  42.7 0.9 broadcast_in_dim.14
  43.6 4.7 %all-to-all-start.1 = ((f32[8,16,1152]{2,1,0:T(8,128)}), f32[8,16,1152]{2,1,0:T(8,128)S(1)}, u32[]{:S(2)}, u32[]{:S(2)}) async-start(f32[8,16,1152]{2,1,0:T(8,128)} %broadcast_in_dim.14), calls=%async_computation.1 | async-start | bytes 1179648 | tf_op jit(solution)/shard_map/all_to_all | solution.py:417
  48.4 9.6 %shard_map.59 = (f32[4,256]{1,0:T(4,128)}, f32[1,256]{1,0:T(1,128)S(1)}, f32[256,256]{1,0:T(8,128)S(1)}, f32[256,256]{1,0:T(8,128)S(1)}) custom-call(f32[64,256]{1,0:T(8,128)S(1)} %bitcast.25, f32[4,256]{1,0:T(4,128)S(1)} %get-tuple-element.18.own_ref.a_ref, f32[256,256]{1,0:T(8,128)S(1)} %get-tuple-element.19.gram_c_ref), custom_call_target="tpu_custom_call" | custom-call | flops 10000000000 | bytes 1000000 | tf_op jit(solution)/shard_map/pallas_call | solution.py:314
  58.0 4.3 %all-to-all-done.1 = f32[8,16,1152]{2,1,0:T(8,128)S(1)} async-done(((f32[8,16,1152]{2,1,0:T(8,128)}), f32[8,16,1152]{2,1,0:T(8,128)S(1)}, u32[]{:S(2)}, u32[]{:S(2)}) %all-to-all-start.1) | async-done | bytes 589856 | tf_op jit(solution)/shard_map/all_to_all | solution.py:417
  62.3 0.0 collective-permute-start.2
  62.3 2.0 %collective-permute-done.2 = f32[8,16,1152]{2,1,0:T(8,128)S(1)} collective-permute-done((f32[8,16,1152]{2,1,0:T(8,128)S(1)}, f32[8,16,1152]{2,1,0:T(8,128)S(1)}, u32[]{:S(2)}, u32[]{:S(2)}) %collective-permute-start.2) | collective-permute-done | bytes 589856 | tf_op jit(solution)/shard_map/ppermute | solution.py:413
  64.3 10.9 %shard_map.60 = (f32[1152,256]{1,0:T(8,128)S(1)}, f32[8,40,256]{2,1,0:T(8,128)S(1)}, f32[8,40,256]{2,1,0:T(8,128)S(1)}) custom-call(f32[4,576,1152]{2,1,0:T(8,128)} %bitcast.34, f32[4,256]{1,0:T(4,128)S(1)} %get-tuple-element.18.own_ref.a_ref, f32[1,256]{1,0:T(1,128)S(1)} %get-tuple-element.21.scale_ref, f32[128,1152]{1,0:T(8,128)S(1)} %bitcast.24, ...), custom_call_target="tpu_custom_call" | custom-call | flops 4076863488 | bytes 10616832 | tf_op jit(solution)/shard_map/pallas_call | solution.py:376
  75.3 0.2 collective-permute-start.3
  75.5 1.5 %collective-permute-done.3 = f32[8,40,256]{2,1,0:T(8,128)S(1)} collective-permute-done((f32[8,40,256]{2,1,0:T(8,128)S(1)}, f32[8,40,256]{2,1,0:T(8,128)S(1)}, u32[]{:S(2)}, u32[]{:S(2)}) %collective-permute-start.3) | collective-permute-done | bytes 327712 | tf_op jit(solution)/shard_map/ppermute | solution.py:413
  76.9 0.8 add.35
  77.7 4.8 %all-to-all-start.2 = ((f32[8,40,256]{2,1,0:T(8,128)}), f32[8,40,256]{2,1,0:T(8,128)S(1)}, u32[]{:S(2)}, u32[]{:S(2)}) async-start(f32[8,40,256]{2,1,0:T(8,128)} %add.35), calls=%async_computation.2 | async-start | bytes 655360 | tf_op jit(solution)/shard_map/all_to_all | solution.py:417
  82.5 9.6 %shard_map.61 = f32[256,256]{1,0:T(8,128)S(1)} custom-call(f32[256,256]{1,0:T(8,128)S(1)} %get-tuple-element.28.a_ref, f32[1152,256]{1,0:T(8,128)S(1)} %get-tuple-element.25.b_ref), custom_call_target="tpu_custom_call" | custom-call | flops 10000000000 | bytes 1000000 | tf_op jit(solution)/shard_map/pallas_call | solution.py:403
  92.1 1.0 all-to-all-done.2
  93.2 0.3 multiply_reduce_fusion
  93.4 0.6 broadcast_in_dim.15
  94.0 5.1 %all-to-all-start.3 = ((f32[16,1,256]{2,1,0:T(1,128)}), f32[16,1,256]{2,1,0:T(1,128)S(1)}, u32[]{:S(2)}, u32[]{:S(2)}) async-start(f32[16,1,256]{2,1,0:T(1,128)} %broadcast_in_dim.15), calls=%async_computation.3 | async-start | bytes 32768 | tf_op jit(solution)/shard_map/all_to_all | solution.py:417
  99.1 0.6 constant_dynamic-slice_fusion
  99.8 5.8 %all-to-all-done.3 = f32[16,1,256]{2,1,0:T(1,128)S(1)} async-done(((f32[16,1,256]{2,1,0:T(1,128)}), f32[16,1,256]{2,1,0:T(1,128)S(1)}, u32[]{:S(2)}, u32[]{:S(2)}) %all-to-all-start.3) | async-done | bytes 16416 | tf_op jit(solution)/shard_map/all_to_all | solution.py:417
  105.7 0.6 broadcast_multiply_fusion
  (15 shorter events, 0.2 us)
Async XLA Ops:
  0.6 1.3 %copy-start = (f32[1152,256]{1,0:T(8,128)S(1)}, f32[1152,256]{1,0:T(8,128)}, u32[]{:S(2)}) copy-start(f32[1152,256]{1,0:T(8,128)} %b_ref.1) | copy-start | bytes 3538948
  1.9 1.1 %copy-start.1 = (f32[576,256]{1,0:T(8,128)S(1)}, f32[576,256]{1,0:T(8,128)}, u32[]{:S(2)}) copy-start(f32[576,256]{1,0:T(8,128)} %c_ref.1) | copy-start | bytes 1769476
  17.4 2.2 %collective-permute-start = (f32[8,16,1280]{2,1,0:T(8,128)S(1)}, f32[8,16,1280]{2,1,0:T(8,128)S(1)}, u32[]{:S(2)}, u32[]{:S(2)}) collective-permute-start(f32[8,16,1280]{2,1,0:T(8,128)S(1)} %get-tuple-element.17), channel_id=1, source_target_pairs={{0,1},{1,0},{2,3},{3,2},{4,5},{5,4},{6,7},{7,6},{8,9},{9,8},{10,11... | collective-permute-start | bytes 1966088 | tf_op jit(solution)/shard_map/ppermute | solution.py:413
  20.5 14.9 %all-to-all-start = ((f32[8,16,1280]{2,1,0:T(8,128)}), f32[8,16,1280]{2,1,0:T(8,128)S(1)}, u32[]{:S(2)}, u32[]{:S(2)}) async-start(f32[8,16,1280]{2,1,0:T(8,128)} %add.30), calls=%async_computation | async-start | bytes 1310720 | tf_op jit(solution)/shard_map/all_to_all | solution.py:417
  35.5 7.2 %collective-permute-start.1 = (f32[1,16,1664]{2,1,0:T(8,128)S(1)}, f32[1,16,1664]{2,1,0:T(8,128)S(1)}, u32[]{:S(2)}, u32[]{:S(2)}) collective-permute-start(f32[1,16,1664]{2,1,0:T(8,128)S(1)} %pad_maximum_fusion), channel_id=1, source_target_pairs={{0,8},{1,9},{2,10},{3,11},{4,12},{5,13},{6,14},{7,15},{8,0},{9,1},... | collective-permute-start | bytes 319496 | tf_op jit(solution)/shard_map/ppermute | solution.py:413
  43.6 18.7 %all-to-all-start.1 = ((f32[8,16,1152]{2,1,0:T(8,128)}), f32[8,16,1152]{2,1,0:T(8,128)S(1)}, u32[]{:S(2)}, u32[]{:S(2)}) async-start(f32[8,16,1152]{2,1,0:T(8,128)} %broadcast_in_dim.14), calls=%async_computation.1 | async-start | bytes 1179648 | tf_op jit(solution)/shard_map/all_to_all | solution.py:417
  62.3 2.0 %collective-permute-start.2 = (f32[8,16,1152]{2,1,0:T(8,128)S(1)}, f32[8,16,1152]{2,1,0:T(8,128)S(1)}, u32[]{:S(2)}, u32[]{:S(2)}) collective-permute-start(f32[8,16,1152]{2,1,0:T(8,128)S(1)} %all-to-all-done.1), channel_id=1, source_target_pairs={{0,1},{1,0},{2,3},{3,2},{4,5},{5,4},{6,7},{7,6},{8,9},{9,8},{10,11... | collective-permute-start | bytes 1769480 | tf_op jit(solution)/shard_map/ppermute | solution.py:413
  75.3 1.7 %collective-permute-start.3 = (f32[8,40,256]{2,1,0:T(8,128)S(1)}, f32[8,40,256]{2,1,0:T(8,128)S(1)}, u32[]{:S(2)}, u32[]{:S(2)}) collective-permute-start(f32[8,40,256]{2,1,0:T(8,128)S(1)} %get-tuple-element.27), channel_id=1, source_target_pairs={{0,1},{1,0},{2,3},{3,2},{4,5},{5,4},{6,7},{7,6},{8,9},{9,8},{10,11... | collective-permute-start | bytes 983048 | tf_op jit(solution)/shard_map/ppermute | solution.py:413
  77.7 15.4 %all-to-all-start.2 = ((f32[8,40,256]{2,1,0:T(8,128)}), f32[8,40,256]{2,1,0:T(8,128)S(1)}, u32[]{:S(2)}, u32[]{:S(2)}) async-start(f32[8,40,256]{2,1,0:T(8,128)} %add.35), calls=%async_computation.2 | async-start | bytes 655360 | tf_op jit(solution)/shard_map/all_to_all | solution.py:417
  94.0 11.6 %all-to-all-start.3 = ((f32[16,1,256]{2,1,0:T(1,128)}), f32[16,1,256]{2,1,0:T(1,128)S(1)}, u32[]{:S(2)}, u32[]{:S(2)}) async-start(f32[16,1,256]{2,1,0:T(1,128)} %broadcast_in_dim.15), calls=%async_computation.3 | async-start | bytes 32768 | tf_op jit(solution)/shard_map/all_to_all | solution.py:417

commit v2 on v1

--- a/solution.py
+++ b/solution.py
@@ -326,7 +326,7 @@
 
 
 def third_kernel(
-    x_hbm, a_ref, scale_ref, own_ref, other_ref, inv_ref, raw_ref, keep_ref, send_ref, x_ref, halves, total, sems
+    x_hbm, a_ref, scale_ref, own_ref, other_ref, inv_ref, raw_ref, gram_ref, keep_ref, send_ref, x_ref, halves, total, sems
 ):
     copies = fetch(x_hbm, x_ref, sems)
     count, depth, width = x_ref.shape
@@ -335,13 +335,17 @@
     mine = inv_ref[pl.ds(pl.multiple_of(core * half, half), half), :]
     others = inv_ref[pl.ds(pl.multiple_of((1 - core) * half, half), half), :]
     raw = mul3(own_ref[...].T, mine) + mul3(other_ref[...].T, others)
-    halves[0], halves[1] = split(raw)
-    row = jnp.sqrt(float(width) / (jnp.sum(raw * raw, axis=0, keepdims=True) + 1e-06))
+    high, low = split(raw)
+    halves[0] = high
+    halves[1] = low
+    turned_high, turned_low = split(raw.T)
+    gram = mul(turned_high, high) + (mul(turned_low, high) + mul(turned_high, low))
+    row, column = scales(gram, float(width))
     raw_ref[...] = raw * row
+    gram_ref[...] = gram * row * column
     both = scale_ref[...] * row
-    for copy in copies:
-        copy.wait()
     for i in range(count):
+        copies[i].wait()
         scale = a_ref[i : i + 1, :] * both
         for at, size in chunks(depth, 192):
             high, low = split(x_ref[i, at : at + size, :])
@@ -376,8 +380,13 @@
     return pl.pallas_call(
         third_kernel,
         in_specs=[pl.BlockSpec(memory_space=pltpu.HBM)] + [vmem] * 5,
-        out_specs=[vmem] * 3,
-        out_shape=[jax.ShapeDtypeStruct((width, rank), jnp.float32), part, part],
+        out_specs=[vmem] * 4,
+        out_shape=[
+            jax.ShapeDtypeStruct((width, rank), jnp.float32),
+            jax.ShapeDtypeStruct((rank, rank), jnp.float32),
+            part,
+            part,
+        ],
         scratch_shapes=[
             pltpu.VMEM((count, depth, width), jnp.float32),
             pltpu.VMEM((2, width, rank), jnp.bfloat16),
@@ -392,20 +401,19 @@
 
 
 def fourth_kernel(a_ref, b_ref, out_ref):
-    b = b_ref[...]
-    matrix, mean = system(a_ref[...], mul3(b.T, b))
+    matrix, mean = system(a_ref[...], b_ref[...])
     out_ref[...] = matrix
     invert(out_ref)
     out_ref[...] = out_ref[...] * (1.0 / mean)
 
 
-def fourth_call(gram_a, all_b):
+def fourth_call(gram_a, gram_b):
     return pl.pallas_call(
         fourth_kernel,
         out_shape=jax.ShapeDtypeStruct(gram_a.shape, jnp.float32),
         compiler_params=pltpu.CompilerParams(vmem_limit_bytes=SMALL),
         cost_estimate=pl.CostEstimate(flops=10**10, bytes_accessed=10**6, transcendentals=0),
-    )(gram_a, all_b)
+    )(gram_a, gram_b)
 
 
 def swap(x, bit):
@@ -424,13 +432,26 @@
     return [[2 * chip + core for chip in order] for core in range(2)]
 
 
-def quads():
+def pass_to(x, mask):
     devices = lax.axis_size("gx")
-    return [
-        [8 * group + core + place for place in (0, 4, 2, 6)]
-        for core in range(2)
-        for group in range(devices // 8)
-    ]
+    return lax.ppermute(x, "gx", [(i, i ^ mask) for i in range(devices)])
+
+
+def quad_scatter(x):
+    me = lax.axis_index("gx")
+    place = ((me >> 1) & 1) * 2 + ((me >> 2) & 1)
+    blocks = [lax.dynamic_index_in_dim(x, place, 0, keepdims=False)]
+    for mask, step in ((2, 2), (4, 1), (6, 3)):
+        blocks.append(pass_to(lax.dynamic_index_in_dim(x, place ^ step, 0, keepdims=False), mask))
+    return blocks
+
+
+def total_of(x):
+    x = x + swap(x, 0)
+    x = (x + pass_to(x, 2)) + (pass_to(x, 4) + pass_to(x, 6))
+    for bit in range(3, lax.axis_size("gx").bit_length() - 1):
+        x = x + swap(x, bit)
+    return x
 
 
 def scatter(keep, send):
@@ -440,9 +461,10 @@
 def halve(keep, send, width):
     me = lax.axis_index("gx")
     x = keep + swap(send, 0)
-    x = exchange(x, quads()).reshape((4, x.shape[0] // 4) + x.shape[1:])
-    tails = x[:, 0, :, width:]
-    x = jnp.sum(x[:, :, :, :width], axis=0)
+    blocks = quad_scatter(x.reshape((4, x.shape[0] // 4) + x.shape[1:]))
+    tails = jnp.concatenate([block[:1, :, width:] for block in blocks], axis=0)
+    first, second, third, fourth = [block[:, :, :width] for block in blocks]
+    x = (first + second) + (third + fourth)
     steps = x.shape[0].bit_length() - 1
     for bit in range(3, steps + 3):
         mine = (me >> bit) & 1
@@ -480,12 +502,6 @@
     return tail.reshape(members * 2 * count, rank)
 
 
-def gather_small(x):
-    devices = lax.axis_size("gx")
-    x = exchange(jnp.broadcast_to(x[None], (devices,) + x.shape), None)
-    return x.reshape((-1,) + x.shape[2:])
-
-
 def local(tensor, factor_b, factor_c):
     devices = lax.axis_size("gx")
     me = lax.axis_index("gx")
@@ -500,15 +516,15 @@
     own, inv_b = lax.optimization_barrier((own, inv_b))
     other = swap(own, 0)
     whole = (rank // 2, total_second)
-    all_b, keep, send = third_call(
+    all_b, gram_b, keep, send = third_call(
         turned, raw_a, scale_a, own.reshape(whole), other.reshape(whole), inv_b, devices
     )
     rows_b = total_second // devices
     new_b = lax.dynamic_slice_in_dim(all_b, me * rows_b, rows_b, axis=0)
-    inv_c = fourth_call(gram_a, all_b)
+    inv_c = fourth_call(gram_a, gram_b)
     side_c = jnp.sum(scatter(keep, send), axis=0)
     raw_c = dot(side_c, inv_c)[: total_third // devices]
-    sums = jnp.sum(gather_small(jnp.sum(raw_c * raw_c, axis=0, keepdims=True)), axis=0)
+    sums = total_of(jnp.sum(raw_c * raw_c, axis=0, keepdims=True))
     new_c = raw_c * jnp.sqrt(total_third / (sums + 1e-06))
     return (new_a, new_b, new_c)
 

time: 107 us -> 104 us (0.972)
  Pallas kernels: 44.4 us -> 42.7 us
  starting transfers between devices: 23.2 us -> 24.3 us
    all_to_all x4 -> x2, waiting for transfers between devices: 20.9 us -> 7.18 us  [exchange(): return lax.all_to_all(x, 'gx', 0, 0, axis_index_groups=groups, tiled=True)]
    ppermute x0 -> x6, waiting for transfers between devices: none -> 9.67 us  [pass_to(): return lax.ppermute(x, 'gx', [(i, i ^ mask) for i in range(devices)])]
    all_to_all x4 -> x2, starting transfers between devices: 19.8 us -> 10.9 us  [exchange(): return lax.all_to_all(x, 'gx', 0, 0, axis_index_groups=groups, tiled=True)]
    ppermute x0 -> x6, starting transfers between devices: none -> 8.1 us  [pass_to(): return lax.ppermute(x, 'gx', [(i, i ^ mask) for i in range(devices)])]
    ppermute x4 -> x6, waiting for transfers between devices: 9.74 us -> 13.6 us  [swap(): return lax.ppermute(x, 'gx', [(i, i ^ 1 << bit) for i in range(devices)])]
    ppermute x4 -> x6, starting transfers between devices: 3.38 us -> 5.31 us  [swap(): return lax.ppermute(x, 'gx', [(i, i ^ 1 << bit) for i in range(devices)])]
    unnamed x5 -> x9, local copies, waits for them, and re-layouts: 2.33 us -> 2.36 us
  transfers between devices with their start and end apart: 8 -> 14, of which waited for: 8 -> 13; matrix products, arithmetic and copies ran while one was open for 1% -> 1% of each run, Pallas kernels for 18% -> 17%
where the time goes in v2:
time: 104 us
  Pallas kernels  42.7 us (41%)
  waiting for transfers between devices  30.5 us (29%)
  starting transfers between devices  24.3 us (23%)
  local copies, waits for them, and re-layouts  4.01 us (4%)
  other arithmetic  1.57 us (2%)
    pallas_call x1, Pallas kernels, first_call(): pl.pallas_call(first_kernel, in_specs=[pl.BlockSpec(memory_space=pltpu.HB...  14.4 us
    ppermute x6, waiting for transfers between devices, swap(): return lax.ppermute(x, 'gx', [(i, i ^ 1 << bit) for i in range(devices)])  13.6 us
    all_to_all x2, starting transfers between devices, exchange(): return lax.all_to_all(x, 'gx', 0, 0, axis_index_groups=groups, tiled=True)  10.9 us
    pallas_call x1, Pallas kernels, third_call(): pl.pallas_call(third_kernel, in_specs=[pl.BlockSpec(memory_space=pltpu.HB...  10.1 us
    ppermute x6, waiting for transfers between devices, pass_to(): return lax.ppermute(x, 'gx', [(i, i ^ mask) for i in range(devices)])  9.67 us
    pallas_call x1, Pallas kernels, second_call(): pl.pallas_call(functools.partial(second_kernel, float(gathered.shape[0]))...  9.56 us
    pallas_call x1, Pallas kernels, fourth_call(): pl.pallas_call(fourth_kernel, out_shape=jax.ShapeDtypeStruct(gram_a.shape...  8.65 us
    ppermute x6, starting transfers between devices, pass_to(): return lax.ppermute(x, 'gx', [(i, i ^ mask) for i in range(devices)])  8.1 us
  transfers between devices with their start and end apart: 14, of which 13 were waited for; matrix products, arithmetic and copies ran while one was open for 1% of the time, Pallas kernels for 17%

profile of v2, /device:TPU:0, one launch (start us, length us, event | category | flops | bytes accessed | tf_op | source)
XLA Modules:
  0.0 104.1 jit_solution(2328164203419757104)
XLA Ops:
  0.6 1.3 %copy-done = f32[1152,256]{1,0:T(8,128)S(1)} copy-done((f32[1152,256]{1,0:T(8,128)S(1)}, f32[1152,256]{1,0:T(8,128)}, u32[]{:S(2)}) %copy-start) | copy-done | bytes 1179672
  1.9 1.1 %copy-done.1 = f32[576,256]{1,0:T(8,128)S(1)} copy-done((f32[576,256]{1,0:T(8,128)S(1)}, f32[576,256]{1,0:T(8,128)}, u32[]{:S(2)}) %copy-start.1) | copy-done | bytes 589848
  3.0 14.4 %shard_map.58 = (f32[4,256]{1,0:T(4,128)S(1)}, f32[8,16,1280]{2,1,0:T(8,128)S(1)}, f32[8,16,1280]{2,1,0:T(8,128)S(1)}, f32[256,256]{1,0:T(8,128)S(1)}) custom-call(f32[4,576,1152]{2,1,0:T(8,128)} %bitcast.48, f32[1152,256]{1,0:T(8,128)S(1)} %copy-done, f32[576,256]{1,0:T(8,128)S(1)} %copy-done.1), custom_call_target="tpu_custom_call" | custom-call | flops 4076863488 | bytes 10616832 | tf_op jit(solution)/shard_map/pallas_call | solution.py:263
  17.4 0.5 collective-permute-start
  17.9 1.7 %collective-permute-done = f32[8,16,1280]{2,1,0:T(8,128)S(1)} collective-permute-done((f32[8,16,1280]{2,1,0:T(8,128)S(1)}, f32[8,16,1280]{2,1,0:T(8,128)S(1)}, u32[]{:S(2)}, u32[]{:S(2)}) %collective-permute-start) | collective-permute-done | bytes 655392 | tf_op jit(solution)/shard_map/ppermute | solution.py:421
  19.7 4.0 %collective-permute-start.3 = (f32[2,16,1280]{2,1,0:T(8,128)S(1)}, f32[2,16,1280]{2,1,0:T(8,128)S(1)}, u32[]{:S(2)}, u32[]{:S(2)}) collective-permute-start(f32[2,16,1280]{2,1,0:T(8,128)S(1)} %get-tuple-element.31), channel_id=1, source_target_pairs={{0,6},{1,7},{2,4},{3,5},{4,2},{5,3},{6,0},{7,1},{8,14},{9,15},{10,... | collective-permute-start | bytes 491528 | tf_op jit(solution)/shard_map/ppermute | solution.py:437
  24.4 4.3 %collective-permute-done.3 = f32[2,16,1280]{2,1,0:T(8,128)S(1)} collective-permute-done((f32[2,16,1280]{2,1,0:T(8,128)S(1)}, f32[2,16,1280]{2,1,0:T(8,128)S(1)}, u32[]{:S(2)}, u32[]{:S(2)}) %collective-permute-start.3) | collective-permute-done | bytes 163872 | tf_op jit(solution)/shard_map/ppermute | solution.py:437
  28.7 3.2 %collective-permute-done.2 = f32[2,16,1280]{2,1,0:T(8,128)S(1)} collective-permute-done((f32[2,16,1280]{2,1,0:T(8,128)S(1)}, f32[2,16,1280]{2,1,0:T(8,128)S(1)}, u32[]{:S(2)}, u32[]{:S(2)}) %collective-permute-start.2) | collective-permute-done | bytes 163872 | tf_op jit(solution)/shard_map/ppermute | solution.py:437
  32.1 2.7 %collective-permute-start.4 = (f32[1,16,1664]{2,1,0:T(8,128)S(1)}, f32[1,16,1664]{2,1,0:T(8,128)S(1)}, u32[]{:S(2)}, u32[]{:S(2)}) collective-permute-start(f32[1,16,1664]{2,1,0:T(8,128)S(1)} %pad_maximum_fusion), channel_id=1, source_target_pairs={{0,8},{1,9},{2,10},{3,11},{4,12},{5,13},{6,14},{7,15},{8,0},{9,1},... | collective-permute-start | bytes 319496 | tf_op jit(solution)/shard_map/ppermute | solution.py:421
  34.7 5.3 %collective-permute-done.4 = f32[1,16,1664]{2,1,0:T(8,128)S(1)} collective-permute-done((f32[1,16,1664]{2,1,0:T(8,128)S(1)}, f32[1,16,1664]{2,1,0:T(8,128)S(1)}, u32[]{:S(2)}, u32[]{:S(2)}) %collective-permute-start.4) | collective-permute-done | bytes 106528 | tf_op jit(solution)/shard_map/ppermute | solution.py:421
  40.0 0.9 broadcast_in_dim.11
  40.9 5.8 %all-to-all-start = ((f32[8,16,1152]{2,1,0:T(8,128)}), f32[8,16,1152]{2,1,0:T(8,128)S(1)}, u32[]{:S(2)}, u32[]{:S(2)}) async-start(f32[8,16,1152]{2,1,0:T(8,128)} %broadcast_in_dim.11), calls=%async_computation | async-start | bytes 1179648 | tf_op jit(solution)/shard_map/all_to_all | solution.py:425
  46.8 9.6 %shard_map.59 = (f32[4,256]{1,0:T(4,128)}, f32[1,256]{1,0:T(1,128)S(1)}, f32[256,256]{1,0:T(8,128)S(1)}, f32[256,256]{1,0:T(8,128)S(1)}) custom-call(f32[64,256]{1,0:T(8,128)S(1)} %bitcast.34, f32[4,256]{1,0:T(4,128)S(1)} %get-tuple-element.19.own_ref.a_ref, f32[256,256]{1,0:T(8,128)S(1)} %get-tuple-element.20.gram_c_ref), custom_call_target="tpu_custom_call" | custom-call | flops 10000000000 | bytes 1000000 | tf_op jit(solution)/shard_map/pallas_call | solution.py:314
  56.3 5.2 %all-to-all-done = f32[8,16,1152]{2,1,0:T(8,128)S(1)} async-done(((f32[8,16,1152]{2,1,0:T(8,128)}), f32[8,16,1152]{2,1,0:T(8,128)S(1)}, u32[]{:S(2)}, u32[]{:S(2)}) %all-to-all-start) | async-done | bytes 589856 | tf_op jit(solution)/shard_map/all_to_all | solution.py:425
  61.6 2.0 %collective-permute-done.5 = f32[8,16,1152]{2,1,0:T(8,128)S(1)} collective-permute-done((f32[8,16,1152]{2,1,0:T(8,128)S(1)}, f32[8,16,1152]{2,1,0:T(8,128)S(1)}, u32[]{:S(2)}, u32[]{:S(2)}) %collective-permute-start.5) | collective-permute-done | bytes 589856 | tf_op jit(solution)/shard_map/ppermute | solution.py:421
  63.6 10.1 %shard_map.60 = (f32[1152,256]{1,0:T(8,128)S(1)}, f32[256,256]{1,0:T(8,128)S(1)}, f32[8,40,256]{2,1,0:T(8,128)S(1)}, f32[8,40,256]{2,1,0:T(8,128)S(1)}) custom-call(f32[4,576,1152]{2,1,0:T(8,128)} %bitcast.49, f32[4,256]{1,0:T(4,128)S(1)} %get-tuple-element.19.own_ref.a_ref, f32[1,256]{1,0:T(1,128)S(1)} %get-tuple-element.22.scale_ref, ...), custom_call_target="tpu_custom_call" | custom-call | flops 4076863488 | bytes 10616832 | tf_op jit(solution)/shard_map/pallas_call | solution.py:380
  73.9 1.5 %collective-permute-done.6 = f32[8,40,256]{2,1,0:T(8,128)S(1)} collective-permute-done((f32[8,40,256]{2,1,0:T(8,128)S(1)}, f32[8,40,256]{2,1,0:T(8,128)S(1)}, u32[]{:S(2)}, u32[]{:S(2)}) %collective-permute-start.6) | collective-permute-done | bytes 327712 | tf_op jit(solution)/shard_map/ppermute | solution.py:421
  75.4 0.8 add.79
  76.1 5.1 %all-to-all-start.1 = ((f32[8,40,256]{2,1,0:T(8,128)}), f32[8,40,256]{2,1,0:T(8,128)S(1)}, u32[]{:S(2)}, u32[]{:S(2)}) async-start(f32[8,40,256]{2,1,0:T(8,128)} %add.79), calls=%async_computation.1 | async-start | bytes 655360 | tf_op jit(solution)/shard_map/all_to_all | solution.py:425
  81.2 8.6 %shard_map.61 = f32[256,256]{1,0:T(8,128)S(1)} custom-call(f32[256,256]{1,0:T(8,128)S(1)} %get-tuple-element.29.a_ref, f32[256,256]{1,0:T(8,128)S(1)} %get-tuple-element.30.b_ref), custom_call_target="tpu_custom_call" | custom-call | flops 10000000000 | bytes 1000000 | tf_op jit(solution)/shard_map/pallas_call | solution.py:411
  89.9 2.0 %all-to-all-done.1 = f32[8,40,256]{2,1,0:T(8,128)S(1)} async-done(((f32[8,40,256]{2,1,0:T(8,128)}), f32[8,40,256]{2,1,0:T(8,128)S(1)}, u32[]{:S(2)}, u32[]{:S(2)}) %all-to-all-start.1) | async-done | bytes 327712 | tf_op jit(solution)/shard_map/all_to_all | solution.py:425
  92.2 1.1 %collective-permute-done.7 = f32[1,256]{1,0:T(1,128)S(1)} collective-permute-done((f32[1,256]{1,0:T(1,128)S(1)}, f32[1,256]{1,0:T(1,128)S(1)}, u32[]{:S(2)}, u32[]{:S(2)}) %collective-permute-start.7) | collective-permute-done | bytes 1056 | tf_op jit(solution)/shard_map/ppermute | solution.py:421
  93.4 1.4 %collective-permute-start.10 = (f32[1,256]{1,0:T(1,128)S(1)}, f32[1,256]{1,0:T(1,128)S(1)}, u32[]{:S(2)}, u32[]{:S(2)}) collective-permute-start(f32[1,256]{1,0:T(1,128)S(1)} %add.80), channel_id=1, source_target_pairs={{0,6},{1,7},{2,4},{3,5},{4,2},{5,3},{6,0},{7,1},{8,14},{9,15},{10,... | collective-permute-start | bytes 3080 | tf_op jit(solution)/shard_map/ppermute | solution.py:437
  94.8 0.6 collective-permute-start.9
  95.4 1.5 %collective-permute-start.8 = (f32[1,256]{1,0:T(1,128)S(1)}, f32[1,256]{1,0:T(1,128)S(1)}, u32[]{:S(2)}, u32[]{:S(2)}) collective-permute-start(f32[1,256]{1,0:T(1,128)S(1)} %add.80), channel_id=1, source_target_pairs={{0,2},{1,3},{2,0},{3,1},{4,6},{5,7},{6,4},{7,5},{8,10},{9,11},{10,... | collective-permute-start | bytes 3080 | tf_op jit(solution)/shard_map/ppermute | solution.py:437
  96.9 1.0 collective-permute-done.10
  97.8 0.5 collective-permute-done.9
  98.3 0.6 collective-permute-done.8
  99.0 1.9 %collective-permute-start.11 = (f32[1,256]{1,0:T(1,128)S(1)}, f32[1,256]{1,0:T(1,128)S(1)}, u32[]{:S(2)}, u32[]{:S(2)}) collective-permute-start(f32[1,256]{1,0:T(1,128)S(1)} %add_add_fusion), channel_id=1, source_target_pairs={{0,8},{1,9},{2,10},{3,11},{4,12},{5,13},{6,14},{7,15},{8,0},{9,1},... | collective-permute-start | bytes 3080 | tf_op jit(solution)/shard_map/ppermute | solution.py:421
  100.8 0.6 constant_dynamic-slice_fusion
  101.5 2.0 %collective-permute-done.11 = f32[1,256]{1,0:T(1,128)S(1)} collective-permute-done((f32[1,256]{1,0:T(1,128)S(1)}, f32[1,256]{1,0:T(1,128)S(1)}, u32[]{:S(2)}, u32[]{:S(2)}) %collective-permute-start.11) | collective-permute-done | bytes 1056 | tf_op jit(solution)/shard_map/ppermute | solution.py:421
  103.4 0.6 broadcast_multiply_fusion
  (35 shorter events, 1.5 us)
Async XLA Ops:
  0.6 1.3 %copy-start = (f32[1152,256]{1,0:T(8,128)S(1)}, f32[1152,256]{1,0:T(8,128)}, u32[]{:S(2)}) copy-start(f32[1152,256]{1,0:T(8,128)} %b_ref.1) | copy-start | bytes 3538948
  1.9 1.1 %copy-start.1 = (f32[576,256]{1,0:T(8,128)S(1)}, f32[576,256]{1,0:T(8,128)}, u32[]{:S(2)}) copy-start(f32[576,256]{1,0:T(8,128)} %c_ref.1) | copy-start | bytes 1769476
  17.4 2.2 %collective-permute-start = (f32[8,16,1280]{2,1,0:T(8,128)S(1)}, f32[8,16,1280]{2,1,0:T(8,128)S(1)}, u32[]{:S(2)}, u32[]{:S(2)}) collective-permute-start(f32[8,16,1280]{2,1,0:T(8,128)S(1)} %get-tuple-element.18), channel_id=1, source_target_pairs={{0,1},{1,0},{2,3},{3,2},{4,5},{5,4},{6,7},{7,6},{8,9},{9,8},{10,11... | collective-permute-start | bytes 1966088 | tf_op jit(solution)/shard_map/ppermute | solution.py:421
  19.7 9.0 %collective-permute-start.3 = (f32[2,16,1280]{2,1,0:T(8,128)S(1)}, f32[2,16,1280]{2,1,0:T(8,128)S(1)}, u32[]{:S(2)}, u32[]{:S(2)}) collective-permute-start(f32[2,16,1280]{2,1,0:T(8,128)S(1)} %get-tuple-element.31), channel_id=1, source_target_pairs={{0,6},{1,7},{2,4},{3,5},{4,2},{5,3},{6,0},{7,1},{8,14},{9,15},{10,... | collective-permute-start | bytes 491528 | tf_op jit(solution)/shard_map/ppermute | solution.py:437
  23.7 8.2 %collective-permute-start.2 = (f32[2,16,1280]{2,1,0:T(8,128)S(1)}, f32[2,16,1280]{2,1,0:T(8,128)S(1)}, u32[]{:S(2)}, u32[]{:S(2)}) collective-permute-start(f32[2,16,1280]{2,1,0:T(8,128)S(1)} %get-tuple-element.32), channel_id=1, source_target_pairs={{0,4},{1,5},{2,6},{3,7},{4,0},{5,1},{6,2},{7,3},{8,12},{9,13},{10,... | collective-permute-start | bytes 491528 | tf_op jit(solution)/shard_map/ppermute | solution.py:437
  24.2 7.8 %collective-permute-start.1 = (f32[2,16,1280]{2,1,0:T(8,128)S(1)}, f32[2,16,1280]{2,1,0:T(8,128)S(1)}, u32[]{:S(2)}, u32[]{:S(2)}) collective-permute-start(f32[2,16,1280]{2,1,0:T(8,128)S(1)} %get-tuple-element.33), channel_id=1, source_target_pairs={{0,2},{1,3},{2,0},{3,1},{4,6},{5,7},{6,4},{7,5},{8,10},{9,11},{10,... | collective-permute-start | bytes 491528 | tf_op jit(solution)/shard_map/ppermute | solution.py:437
  32.1 8.0 %collective-permute-start.4 = (f32[1,16,1664]{2,1,0:T(8,128)S(1)}, f32[1,16,1664]{2,1,0:T(8,128)S(1)}, u32[]{:S(2)}, u32[]{:S(2)}) collective-permute-start(f32[1,16,1664]{2,1,0:T(8,128)S(1)} %pad_maximum_fusion), channel_id=1, source_target_pairs={{0,8},{1,9},{2,10},{3,11},{4,12},{5,13},{6,14},{7,15},{8,0},{9,1},... | collective-permute-start | bytes 319496 | tf_op jit(solution)/shard_map/ppermute | solution.py:421
  40.9 20.6 %all-to-all-start = ((f32[8,16,1152]{2,1,0:T(8,128)}), f32[8,16,1152]{2,1,0:T(8,128)S(1)}, u32[]{:S(2)}, u32[]{:S(2)}) async-start(f32[8,16,1152]{2,1,0:T(8,128)} %broadcast_in_dim.11), calls=%async_computation | async-start | bytes 1179648 | tf_op jit(solution)/shard_map/all_to_all | solution.py:425
  61.6 2.0 %collective-permute-start.5 = (f32[8,16,1152]{2,1,0:T(8,128)S(1)}, f32[8,16,1152]{2,1,0:T(8,128)S(1)}, u32[]{:S(2)}, u32[]{:S(2)}) collective-permute-start(f32[8,16,1152]{2,1,0:T(8,128)S(1)} %all-to-all-done), channel_id=1, source_target_pairs={{0,1},{1,0},{2,3},{3,2},{4,5},{5,4},{6,7},{7,6},{8,9},{9,8},{10,11... | collective-permute-start | bytes 1769480 | tf_op jit(solution)/shard_map/ppermute | solution.py:421
  73.7 1.7 %collective-permute-start.6 = (f32[8,40,256]{2,1,0:T(8,128)S(1)}, f32[8,40,256]{2,1,0:T(8,128)S(1)}, u32[]{:S(2)}, u32[]{:S(2)}) collective-permute-start(f32[8,40,256]{2,1,0:T(8,128)S(1)} %get-tuple-element.28), channel_id=1, source_target_pairs={{0,1},{1,0},{2,3},{3,2},{4,5},{5,4},{6,7},{7,6},{8,9},{9,8},{10,11... | collective-permute-start | bytes 983048 | tf_op jit(solution)/shard_map/ppermute | solution.py:421
  76.1 15.7 %all-to-all-start.1 = ((f32[8,40,256]{2,1,0:T(8,128)}), f32[8,40,256]{2,1,0:T(8,128)S(1)}, u32[]{:S(2)}, u32[]{:S(2)}) async-start(f32[8,40,256]{2,1,0:T(8,128)} %add.79), calls=%async_computation.1 | async-start | bytes 655360 | tf_op jit(solution)/shard_map/all_to_all | solution.py:425
  92.2 1.2 %collective-permute-start.7 = (f32[1,256]{1,0:T(1,128)S(1)}, f32[1,256]{1,0:T(1,128)S(1)}, u32[]{:S(2)}, u32[]{:S(2)}) collective-permute-start(f32[1,256]{1,0:T(1,128)S(1)} %bitcast.45), channel_id=1, source_target_pairs={{0,1},{1,0},{2,3},{3,2},{4,5},{5,4},{6,7},{7,6},{8,9},{9,8},{10,11... | collective-permute-start | bytes 3080 | tf_op jit(solution)/shard_map/ppermute | solution.py:421
  93.4 4.5 %collective-permute-start.10 = (f32[1,256]{1,0:T(1,128)S(1)}, f32[1,256]{1,0:T(1,128)S(1)}, u32[]{:S(2)}, u32[]{:S(2)}) collective-permute-start(f32[1,256]{1,0:T(1,128)S(1)} %add.80), channel_id=1, source_target_pairs={{0,6},{1,7},{2,4},{3,5},{4,2},{5,3},{6,0},{7,1},{8,14},{9,15},{10,... | collective-permute-start | bytes 3080 | tf_op jit(solution)/shard_map/ppermute | solution.py:437
  94.8 3.6 %collective-permute-start.9 = (f32[1,256]{1,0:T(1,128)S(1)}, f32[1,256]{1,0:T(1,128)S(1)}, u32[]{:S(2)}, u32[]{:S(2)}) collective-permute-start(f32[1,256]{1,0:T(1,128)S(1)} %add.80), channel_id=1, source_target_pairs={{0,4},{1,5},{2,6},{3,7},{4,0},{5,1},{6,2},{7,3},{8,12},{9,13},{10,... | collective-permute-start | bytes 3080 | tf_op jit(solution)/shard_map/ppermute | solution.py:437
  95.4 3.6 %collective-permute-start.8 = (f32[1,256]{1,0:T(1,128)S(1)}, f32[1,256]{1,0:T(1,128)S(1)}, u32[]{:S(2)}, u32[]{:S(2)}) collective-permute-start(f32[1,256]{1,0:T(1,128)S(1)} %add.80), channel_id=1, source_target_pairs={{0,2},{1,3},{2,0},{3,1},{4,6},{5,7},{6,4},{7,5},{8,10},{9,11},{10,... | collective-permute-start | bytes 3080 | tf_op jit(solution)/shard_map/ppermute | solution.py:437
  99.0 4.5 %collective-permute-start.11 = (f32[1,256]{1,0:T(1,128)S(1)}, f32[1,256]{1,0:T(1,128)S(1)}, u32[]{:S(2)}, u32[]{:S(2)}) collective-permute-start(f32[1,256]{1,0:T(1,128)S(1)} %add_add_fusion), channel_id=1, source_target_pairs={{0,8},{1,9},{2,10},{3,11},{4,12},{5,13},{6,14},{7,15},{8,0},{9,1},... | collective-permute-start | bytes 3080 | tf_op jit(solution)/shard_map/ppermute | solution.py:421

commit v3 on v2

--- a/solution.py
+++ b/solution.py
@@ -491,8 +491,28 @@
 
 
 def spread_out(x):
-    members = lax.axis_size("gx") // 2
-    return exchange(jnp.broadcast_to(x[None], (members,) + x.shape), chips())
+    me = lax.axis_index("gx")
+    x = x[None]
+    for bit in reversed(range(3, lax.axis_size("gx").bit_length() - 1)):
+        other = swap(x, bit)
+        x = jnp.where(
+            (me >> bit) & 1 == 0,
+            jnp.concatenate([x, other], axis=0),
+            jnp.concatenate([other, x], axis=0),
+        )
+    far, near, both = pass_to(x, 4), pass_to(x, 2), pass_to(x, 6)
+    is_far, is_near = (me >> 2) & 1 == 1, (me >> 1) & 1 == 1
+    mine = jnp.where(
+        is_far, jnp.concatenate([far, x], axis=0), jnp.concatenate([x, far], axis=0)
+    )
+    others = jnp.where(
+        is_far, jnp.concatenate([both, near], axis=0), jnp.concatenate([near, both], axis=0)
+    )
+    return jnp.where(
+        is_near,
+        jnp.concatenate([others, mine], axis=0),
+        jnp.concatenate([mine, others], axis=0),
+    )
 
 
 def unpack(tail, count, rank):

time: 104 us -> 107 us (1.029)
  waiting for transfers between devices: 30.5 us -> 36.3 us
  starting transfers between devices: 24.3 us -> 21.5 us
    all_to_all x2 -> x1, starting transfers between devices: 10.9 us -> 4.01 us  [exchange(): return lax.all_to_all(x, 'gx', 0, 0, axis_index_groups=groups, tiled=True)]
    ppermute x6 -> x7, waiting for transfers between devices: 13.6 us -> 19.9 us  [swap(): return lax.ppermute(x, 'gx', [(i, i ^ 1 << bit) for i in range(devices)])]
    all_to_all x2 -> x1, waiting for transfers between devices: 7.18 us -> 1.97 us  [exchange(): return lax.all_to_all(x, 'gx', 0, 0, axis_index_groups=groups, tiled=True)]
    ppermute x6 -> x9, waiting for transfers between devices: 9.67 us -> 14.5 us  [pass_to(): return lax.ppermute(x, 'gx', [(i, i ^ mask) for i in range(devices)])]
    ppermute x6 -> x9, starting transfers between devices: 8.1 us -> 11.6 us  [pass_to(): return lax.ppermute(x, 'gx', [(i, i ^ mask) for i in range(devices)])]
    ppermute x6 -> x7, starting transfers between devices: 5.31 us -> 5.9 us  [swap(): return lax.ppermute(x, 'gx', [(i, i ^ 1 << bit) for i in range(devices)])]
  transfers between devices with their start and end apart: 14 -> 17, of which waited for: 13 -> 14; matrix products, arithmetic and copies ran while one was open for 1% -> 1% of each run, Pallas kernels for 17% -> 17%
where the time goes in v3:
time: 107 us; the launch traced here: 106 us
  Pallas kernels  42.7 us (40%)
  waiting for transfers between devices  36.3 us (34%)
  starting transfers between devices  21.5 us (20%)
  local copies, waits for them, and re-layouts  3.12 us (3%)
  other arithmetic  1.71 us (2%)
    ppermute x7, waiting for transfers between devices, swap(): return lax.ppermute(x, 'gx', [(i, i ^ 1 << bit) for i in range(devices)])  19.9 us
    ppermute x9, waiting for transfers between devices, pass_to(): return lax.ppermute(x, 'gx', [(i, i ^ mask) for i in range(devices)])  14.5 us
    pallas_call x1, Pallas kernels, first_call(): pl.pallas_call(first_kernel, in_specs=[pl.BlockSpec(memory_space=pltpu.HB...  14.4 us
    ppermute x9, starting transfers between devices, pass_to(): return lax.ppermute(x, 'gx', [(i, i ^ mask) for i in range(devices)])  11.6 us
    pallas_call x1, Pallas kernels, third_call(): pl.pallas_call(third_kernel, in_specs=[pl.BlockSpec(memory_space=pltpu.HB...  10.1 us
    pallas_call x1, Pallas kernels, second_call(): pl.pallas_call(functools.partial(second_kernel, float(gathered.shape[0]))...  9.56 us
    pallas_call x1, Pallas kernels, fourth_call(): pl.pallas_call(fourth_kernel, out_shape=jax.ShapeDtypeStruct(gram_a.shape...  8.65 us
    ppermute x7, starting transfers between devices, swap(): return lax.ppermute(x, 'gx', [(i, i ^ 1 << bit) for i in range(devices)])  5.9 us
  transfers between devices with their start and end apart: 17, of which 14 were waited for; matrix products, arithmetic and copies ran while one was open for 1% of the time, Pallas kernels for 17%

profile of v3, /device:TPU:0, one launch (start us, length us, event | category | flops | bytes accessed | tf_op | source)
XLA Modules:
  0.0 106.5 jit_solution(15389952056162880626)
XLA Ops:
  0.6 1.3 %copy-done = f32[1152,256]{1,0:T(8,128)S(1)} copy-done((f32[1152,256]{1,0:T(8,128)S(1)}, f32[1152,256]{1,0:T(8,128)}, u32[]{:S(2)}) %copy-start) | copy-done | bytes 1179672
  1.9 1.1 copy-done.1
  3.0 14.4 %shard_map.58 = (f32[4,256]{1,0:T(4,128)S(1)}, f32[8,16,1280]{2,1,0:T(8,128)S(1)}, f32[8,16,1280]{2,1,0:T(8,128)S(1)}, f32[256,256]{1,0:T(8,128)S(1)}) custom-call(f32[4,576,1152]{2,1,0:T(8,128)} %bitcast.47, f32[1152,256]{1,0:T(8,128)S(1)} %copy-done, f32[576,256]{1,0:T(8,128)S(1)} %copy-done.1), custom_call_target="tpu_custom_call" | custom-call | flops 4076863488 | bytes 10616832 | tf_op jit(solution)/shard_map/pallas_call | solution.py:263
  17.9 1.7 %collective-permute-done = f32[8,16,1280]{2,1,0:T(8,128)S(1)} collective-permute-done((f32[8,16,1280]{2,1,0:T(8,128)S(1)}, f32[8,16,1280]{2,1,0:T(8,128)S(1)}, u32[]{:S(2)}, u32[]{:S(2)}) %collective-permute-start) | collective-permute-done | bytes 655392 | tf_op jit(solution)/shard_map/ppermute | solution.py:421
  19.8 4.0 %collective-permute-start.3 = (f32[2,16,1280]{2,1,0:T(8,128)S(1)}, f32[2,16,1280]{2,1,0:T(8,128)S(1)}, u32[]{:S(2)}, u32[]{:S(2)}) collective-permute-start(f32[2,16,1280]{2,1,0:T(8,128)S(1)} %get-tuple-element.31), channel_id=1, source_target_pairs={{0,6},{1,7},{2,4},{3,5},{4,2},{5,3},{6,0},{7,1},{8,14},{9,15},{10,... | collective-permute-start | bytes 491528 | tf_op jit(solution)/shard_map/ppermute | solution.py:437
  24.4 4.3 %collective-permute-done.3 = f32[2,16,1280]{2,1,0:T(8,128)S(1)} collective-permute-done((f32[2,16,1280]{2,1,0:T(8,128)S(1)}, f32[2,16,1280]{2,1,0:T(8,128)S(1)}, u32[]{:S(2)}, u32[]{:S(2)}) %collective-permute-start.3) | collective-permute-done | bytes 163872 | tf_op jit(solution)/shard_map/ppermute | solution.py:437
  28.7 3.2 %collective-permute-done.2 = f32[2,16,1280]{2,1,0:T(8,128)S(1)} collective-permute-done((f32[2,16,1280]{2,1,0:T(8,128)S(1)}, f32[2,16,1280]{2,1,0:T(8,128)S(1)}, u32[]{:S(2)}, u32[]{:S(2)}) %collective-permute-start.2) | collective-permute-done | bytes 163872 | tf_op jit(solution)/shard_map/ppermute | solution.py:437
  32.1 2.7 %collective-permute-start.4 = (f32[1,16,1664]{2,1,0:T(8,128)S(1)}, f32[1,16,1664]{2,1,0:T(8,128)S(1)}, u32[]{:S(2)}, u32[]{:S(2)}) collective-permute-start(f32[1,16,1664]{2,1,0:T(8,128)S(1)} %pad_maximum_fusion), channel_id=1, source_target_pairs={{0,8},{1,9},{2,10},{3,11},{4,12},{5,13},{6,14},{7,15},{8,0},{9,1},... | collective-permute-start | bytes 319496 | tf_op jit(solution)/shard_map/ppermute | solution.py:421
  34.8 5.3 %collective-permute-done.4 = f32[1,16,1664]{2,1,0:T(8,128)S(1)} collective-permute-done((f32[1,16,1664]{2,1,0:T(8,128)S(1)}, f32[1,16,1664]{2,1,0:T(8,128)S(1)}, u32[]{:S(2)}, u32[]{:S(2)}) %collective-permute-start.4) | collective-permute-done | bytes 106528 | tf_op jit(solution)/shard_map/ppermute | solution.py:421
  40.1 0.5 collective-permute-start.5
  40.6 6.3 %collective-permute-done.5 = f32[1,16,1152]{2,1,0:T(8,128)S(1)} collective-permute-done((f32[1,16,1152]{2,1,0:T(8,128)S(1)}, f32[1,16,1152]{2,1,0:T(8,128)S(1)}, u32[]{:S(2)}, u32[]{:S(2)}) %collective-permute-start.5) | collective-permute-done | bytes 73760 | tf_op jit(solution)/shard_map/ppermute | solution.py:421
  47.0 9.6 %shard_map.59 = (f32[4,256]{1,0:T(4,128)}, f32[1,256]{1,0:T(1,128)S(1)}, f32[256,256]{1,0:T(8,128)S(1)}, f32[256,256]{1,0:T(8,128)S(1)}) custom-call(f32[64,256]{1,0:T(8,128)S(1)} %bitcast.35, f32[4,256]{1,0:T(4,128)S(1)} %get-tuple-element.19.own_ref.a_ref, f32[256,256]{1,0:T(8,128)S(1)} %get-tuple-element.20.gram_c_ref), custom_call_target="tpu_custom_call" | custom-call | flops 10000000000 | bytes 1000000 | tf_op jit(solution)/shard_map/pallas_call | solution.py:314
  56.6 1.5 %collective-permute-start.7 = (f32[2,16,1152]{2,1,0:T(8,128)S(1)}, f32[2,16,1152]{2,1,0:T(8,128)S(1)}, u32[]{:S(2)}, u32[]{:S(2)}) collective-permute-start(f32[2,16,1152]{2,1,0:T(8,128)S(1)} %maximum_select_fusion.3), channel_id=1, source_target_pairs={{0,2},{1,3},{2,0},{3,1},{4,6},{5,7},{6,4},{7,5},{8,10},{9,11},{10,... | collective-permute-start | bytes 442376 | tf_op jit(solution)/shard_map/ppermute | solution.py:437
  58.1 1.9 %collective-permute-start.6 = (f32[2,16,1152]{2,1,0:T(8,128)S(1)}, f32[2,16,1152]{2,1,0:T(8,128)S(1)}, u32[]{:S(2)}, u32[]{:S(2)}) collective-permute-start(f32[2,16,1152]{2,1,0:T(8,128)S(1)} %maximum_select_fusion.3), channel_id=1, source_target_pairs={{0,6},{1,7},{2,4},{3,5},{4,2},{5,3},{6,0},{7,1},{8,14},{9,15},{10,... | collective-permute-start | bytes 442376 | tf_op jit(solution)/shard_map/ppermute | solution.py:437
  60.1 4.8 %collective-permute-done.7 = f32[2,16,1152]{2,1,0:T(8,128)S(1)} collective-permute-done((f32[2,16,1152]{2,1,0:T(8,128)S(1)}, f32[2,16,1152]{2,1,0:T(8,128)S(1)}, u32[]{:S(2)}, u32[]{:S(2)}) %collective-permute-start.7) | collective-permute-done | bytes 147488 | tf_op jit(solution)/shard_map/ppermute | solution.py:437
  65.0 2.0 %collective-permute-done.9 = f32[8,16,1152]{2,1,0:T(8,128)S(1)} collective-permute-done((f32[8,16,1152]{2,1,0:T(8,128)S(1)}, f32[8,16,1152]{2,1,0:T(8,128)S(1)}, u32[]{:S(2)}, u32[]{:S(2)}) %collective-permute-start.9) | collective-permute-done | bytes 589856 | tf_op jit(solution)/shard_map/ppermute | solution.py:421
  67.0 10.1 %shard_map.60 = (f32[1152,256]{1,0:T(8,128)S(1)}, f32[256,256]{1,0:T(8,128)S(1)}, f32[8,40,256]{2,1,0:T(8,128)S(1)}, f32[8,40,256]{2,1,0:T(8,128)S(1)}) custom-call(f32[4,576,1152]{2,1,0:T(8,128)} %bitcast.48, f32[4,256]{1,0:T(4,128)S(1)} %get-tuple-element.19.own_ref.a_ref, f32[1,256]{1,0:T(1,128)S(1)} %get-tuple-element.22.scale_ref, ...), custom_call_target="tpu_custom_call" | custom-call | flops 4076863488 | bytes 10616832 | tf_op jit(solution)/shard_map/pallas_call | solution.py:380
  77.3 1.5 %collective-permute-done.10 = f32[8,40,256]{2,1,0:T(8,128)S(1)} collective-permute-done((f32[8,40,256]{2,1,0:T(8,128)S(1)}, f32[8,40,256]{2,1,0:T(8,128)S(1)}, u32[]{:S(2)}, u32[]{:S(2)}) %collective-permute-start.10) | collective-permute-done | bytes 327712 | tf_op jit(solution)/shard_map/ppermute | solution.py:421
  78.8 0.8 add.79
  79.6 4.0 %all-to-all-start = ((f32[8,40,256]{2,1,0:T(8,128)}), f32[8,40,256]{2,1,0:T(8,128)S(1)}, u32[]{:S(2)}, u32[]{:S(2)}) async-start(f32[8,40,256]{2,1,0:T(8,128)} %add.79), calls=%async_computation | async-start | bytes 655360 | tf_op jit(solution)/shard_map/all_to_all | solution.py:425
  83.6 8.6 %shard_map.61 = f32[256,256]{1,0:T(8,128)S(1)} custom-call(f32[256,256]{1,0:T(8,128)S(1)} %get-tuple-element.29.a_ref, f32[256,256]{1,0:T(8,128)S(1)} %get-tuple-element.30.b_ref), custom_call_target="tpu_custom_call" | custom-call | flops 10000000000 | bytes 1000000 | tf_op jit(solution)/shard_map/pallas_call | solution.py:411
  92.3 2.0 %all-to-all-done = f32[8,40,256]{2,1,0:T(8,128)S(1)} async-done(((f32[8,40,256]{2,1,0:T(8,128)}), f32[8,40,256]{2,1,0:T(8,128)S(1)}, u32[]{:S(2)}, u32[]{:S(2)}) %all-to-all-start) | async-done | bytes 327712 | tf_op jit(solution)/shard_map/all_to_all | solution.py:425
  94.6 1.1 %collective-permute-done.11 = f32[1,256]{1,0:T(1,128)S(1)} collective-permute-done((f32[1,256]{1,0:T(1,128)S(1)}, f32[1,256]{1,0:T(1,128)S(1)}, u32[]{:S(2)}, u32[]{:S(2)}) %collective-permute-start.11) | collective-permute-done | bytes 1056 | tf_op jit(solution)/shard_map/ppermute | solution.py:421
  95.7 1.4 %collective-permute-start.14 = (f32[1,256]{1,0:T(1,128)S(1)}, f32[1,256]{1,0:T(1,128)S(1)}, u32[]{:S(2)}, u32[]{:S(2)}) collective-permute-start(f32[1,256]{1,0:T(1,128)S(1)} %add.80), channel_id=1, source_target_pairs={{0,6},{1,7},{2,4},{3,5},{4,2},{5,3},{6,0},{7,1},{8,14},{9,15},{10,... | collective-permute-start | bytes 3080 | tf_op jit(solution)/shard_map/ppermute | solution.py:437
  97.2 0.6 collective-permute-start.13
  97.8 1.5 %collective-permute-start.12 = (f32[1,256]{1,0:T(1,128)S(1)}, f32[1,256]{1,0:T(1,128)S(1)}, u32[]{:S(2)}, u32[]{:S(2)}) collective-permute-start(f32[1,256]{1,0:T(1,128)S(1)} %add.80), channel_id=1, source_target_pairs={{0,2},{1,3},{2,0},{3,1},{4,6},{5,7},{6,4},{7,5},{8,10},{9,11},{10,... | collective-permute-start | bytes 3080 | tf_op jit(solution)/shard_map/ppermute | solution.py:437
  99.2 1.0 collective-permute-done.14
  100.7 0.6 collective-permute-done.12
  101.3 1.9 %collective-permute-start.15 = (f32[1,256]{1,0:T(1,128)S(1)}, f32[1,256]{1,0:T(1,128)S(1)}, u32[]{:S(2)}, u32[]{:S(2)}) collective-permute-start(f32[1,256]{1,0:T(1,128)S(1)} %add_add_fusion), channel_id=1, source_target_pairs={{0,8},{1,9},{2,10},{3,11},{4,12},{5,13},{6,14},{7,15},{8,0},{9,1},... | collective-permute-start | bytes 3080 | tf_op jit(solution)/shard_map/ppermute | solution.py:421
  103.2 0.6 constant_dynamic-slice_fusion
  103.8 2.0 %collective-permute-done.15 = f32[1,256]{1,0:T(1,128)S(1)} collective-permute-done((f32[1,256]{1,0:T(1,128)S(1)}, f32[1,256]{1,0:T(1,128)S(1)}, u32[]{:S(2)}, u32[]{:S(2)}) %collective-permute-start.15) | collective-permute-done | bytes 1056 | tf_op jit(solution)/shard_map/ppermute | solution.py:421
  105.8 0.6 broadcast_multiply_fusion
  (41 shorter events, 2.8 us)
Async XLA Ops:
  0.6 1.3 %copy-start = (f32[1152,256]{1,0:T(8,128)S(1)}, f32[1152,256]{1,0:T(8,128)}, u32[]{:S(2)}) copy-start(f32[1152,256]{1,0:T(8,128)} %b_ref.1) | copy-start | bytes 3538948
  1.9 1.1 copy-start.1
  17.4 2.2 %collective-permute-start = (f32[8,16,1280]{2,1,0:T(8,128)S(1)}, f32[8,16,1280]{2,1,0:T(8,128)S(1)}, u32[]{:S(2)}, u32[]{:S(2)}) collective-permute-start(f32[8,16,1280]{2,1,0:T(8,128)S(1)} %get-tuple-element.18), channel_id=1, source_target_pairs={{0,1},{1,0},{2,3},{3,2},{4,5},{5,4},{6,7},{7,6},{8,9},{9,8},{10,11... | collective-permute-start | bytes 1966088 | tf_op jit(solution)/shard_map/ppermute | solution.py:421
  19.8 9.0 %collective-permute-start.3 = (f32[2,16,1280]{2,1,0:T(8,128)S(1)}, f32[2,16,1280]{2,1,0:T(8,128)S(1)}, u32[]{:S(2)}, u32[]{:S(2)}) collective-permute-start(f32[2,16,1280]{2,1,0:T(8,128)S(1)} %get-tuple-element.31), channel_id=1, source_target_pairs={{0,6},{1,7},{2,4},{3,5},{4,2},{5,3},{6,0},{7,1},{8,14},{9,15},{10,... | collective-permute-start | bytes 491528 | tf_op jit(solution)/shard_map/ppermute | solution.py:437
  23.7 8.2 %collective-permute-start.2 = (f32[2,16,1280]{2,1,0:T(8,128)S(1)}, f32[2,16,1280]{2,1,0:T(8,128)S(1)}, u32[]{:S(2)}, u32[]{:S(2)}) collective-permute-start(f32[2,16,1280]{2,1,0:T(8,128)S(1)} %get-tuple-element.32), channel_id=1, source_target_pairs={{0,4},{1,5},{2,6},{3,7},{4,0},{5,1},{6,2},{7,3},{8,12},{9,13},{10,... | collective-permute-start | bytes 491528 | tf_op jit(solution)/shard_map/ppermute | solution.py:437
  24.2 7.8 %collective-permute-start.1 = (f32[2,16,1280]{2,1,0:T(8,128)S(1)}, f32[2,16,1280]{2,1,0:T(8,128)S(1)}, u32[]{:S(2)}, u32[]{:S(2)}) collective-permute-start(f32[2,16,1280]{2,1,0:T(8,128)S(1)} %get-tuple-element.33), channel_id=1, source_target_pairs={{0,2},{1,3},{2,0},{3,1},{4,6},{5,7},{6,4},{7,5},{8,10},{9,11},{10,... | collective-permute-start | bytes 491528 | tf_op jit(solution)/shard_map/ppermute | solution.py:437
  32.1 8.0 %collective-permute-start.4 = (f32[1,16,1664]{2,1,0:T(8,128)S(1)}, f32[1,16,1664]{2,1,0:T(8,128)S(1)}, u32[]{:S(2)}, u32[]{:S(2)}) collective-permute-start(f32[1,16,1664]{2,1,0:T(8,128)S(1)} %pad_maximum_fusion), channel_id=1, source_target_pairs={{0,8},{1,9},{2,10},{3,11},{4,12},{5,13},{6,14},{7,15},{8,0},{9,1},... | collective-permute-start | bytes 319496 | tf_op jit(solution)/shard_map/ppermute | solution.py:421
  40.1 6.8 %collective-permute-start.5 = (f32[1,16,1152]{2,1,0:T(8,128)S(1)}, f32[1,16,1152]{2,1,0:T(8,128)S(1)}, u32[]{:S(2)}, u32[]{:S(2)}) collective-permute-start(f32[1,16,1152]{2,1,0:T(8,128)S(1)} %slice_add_fusion.2), channel_id=1, source_target_pairs={{0,8},{1,9},{2,10},{3,11},{4,12},{5,13},{6,14},{7,15},{8,0},{9,1},... | collective-permute-start | bytes 221192 | tf_op jit(solution)/shard_map/ppermute | solution.py:421
  46.9 13.1 %collective-permute-start.8 = (f32[2,16,1152]{2,1,0:T(8,128)S(1)}, f32[2,16,1152]{2,1,0:T(8,128)S(1)}, u32[]{:S(2)}, u32[]{:S(2)}) collective-permute-start(f32[2,16,1152]{2,1,0:T(8,128)S(1)} %maximum_select_fusion.3), channel_id=1, source_target_pairs={{0,4},{1,5},{2,6},{3,7},{4,0},{5,1},{6,2},{7,3},{8,12},{9,13},{10,... | collective-permute-start | bytes 442376 | tf_op jit(solution)/shard_map/ppermute | solution.py:437
  56.6 8.3 %collective-permute-start.7 = (f32[2,16,1152]{2,1,0:T(8,128)S(1)}, f32[2,16,1152]{2,1,0:T(8,128)S(1)}, u32[]{:S(2)}, u32[]{:S(2)}) collective-permute-start(f32[2,16,1152]{2,1,0:T(8,128)S(1)} %maximum_select_fusion.3), channel_id=1, source_target_pairs={{0,2},{1,3},{2,0},{3,1},{4,6},{5,7},{6,4},{7,5},{8,10},{9,11},{10,... | collective-permute-start | bytes 442376 | tf_op jit(solution)/shard_map/ppermute | solution.py:437
  58.1 6.8 %collective-permute-start.6 = (f32[2,16,1152]{2,1,0:T(8,128)S(1)}, f32[2,16,1152]{2,1,0:T(8,128)S(1)}, u32[]{:S(2)}, u32[]{:S(2)}) collective-permute-start(f32[2,16,1152]{2,1,0:T(8,128)S(1)} %maximum_select_fusion.3), channel_id=1, source_target_pairs={{0,6},{1,7},{2,4},{3,5},{4,2},{5,3},{6,0},{7,1},{8,14},{9,15},{10,... | collective-permute-start | bytes 442376 | tf_op jit(solution)/shard_map/ppermute | solution.py:437
  65.0 2.1 %collective-permute-start.9 = (f32[8,16,1152]{2,1,0:T(8,128)S(1)}, f32[8,16,1152]{2,1,0:T(8,128)S(1)}, u32[]{:S(2)}, u32[]{:S(2)}) collective-permute-start(f32[8,16,1152]{2,1,0:T(8,128)S(1)} %maximum_select_fusion), channel_id=1, source_target_pairs={{0,1},{1,0},{2,3},{3,2},{4,5},{5,4},{6,7},{7,6},{8,9},{9,8},{10,11... | collective-permute-start | bytes 1769480 | tf_op jit(solution)/shard_map/ppermute | solution.py:421
  77.2 1.7 %collective-permute-start.10 = (f32[8,40,256]{2,1,0:T(8,128)S(1)}, f32[8,40,256]{2,1,0:T(8,128)S(1)}, u32[]{:S(2)}, u32[]{:S(2)}) collective-permute-start(f32[8,40,256]{2,1,0:T(8,128)S(1)} %get-tuple-element.28), channel_id=1, source_target_pairs={{0,1},{1,0},{2,3},{3,2},{4,5},{5,4},{6,7},{7,6},{8,9},{9,8},{10,11... | collective-permute-start | bytes 983048 | tf_op jit(solution)/shard_map/ppermute | solution.py:421
  79.6 14.6 %all-to-all-start = ((f32[8,40,256]{2,1,0:T(8,128)}), f32[8,40,256]{2,1,0:T(8,128)S(1)}, u32[]{:S(2)}, u32[]{:S(2)}) async-start(f32[8,40,256]{2,1,0:T(8,128)} %add.79), calls=%async_computation | async-start | bytes 655360 | tf_op jit(solution)/shard_map/all_to_all | solution.py:425
  94.5 1.2 %collective-permute-start.11 = (f32[1,256]{1,0:T(1,128)S(1)}, f32[1,256]{1,0:T(1,128)S(1)}, u32[]{:S(2)}, u32[]{:S(2)}) collective-permute-start(f32[1,256]{1,0:T(1,128)S(1)} %bitcast.44), channel_id=1, source_target_pairs={{0,1},{1,0},{2,3},{3,2},{4,5},{5,4},{6,7},{7,6},{8,9},{9,8},{10,11... | collective-permute-start | bytes 3080 | tf_op jit(solution)/shard_map/ppermute | solution.py:421
  95.7 4.5 %collective-permute-start.14 = (f32[1,256]{1,0:T(1,128)S(1)}, f32[1,256]{1,0:T(1,128)S(1)}, u32[]{:S(2)}, u32[]{:S(2)}) collective-permute-start(f32[1,256]{1,0:T(1,128)S(1)} %add.80), channel_id=1, source_target_pairs={{0,6},{1,7},{2,4},{3,5},{4,2},{5,3},{6,0},{7,1},{8,14},{9,15},{10,... | collective-permute-start | bytes 3080 | tf_op jit(solution)/shard_map/ppermute | solution.py:437
  97.2 3.6 %collective-permute-start.13 = (f32[1,256]{1,0:T(1,128)S(1)}, f32[1,256]{1,0:T(1,128)S(1)}, u32[]{:S(2)}, u32[]{:S(2)}) collective-permute-start(f32[1,256]{1,0:T(1,128)S(1)} %add.80), channel_id=1, source_target_pairs={{0,4},{1,5},{2,6},{3,7},{4,0},{5,1},{6,2},{7,3},{8,12},{9,13},{10,... | collective-permute-start | bytes 3080 | tf_op jit(solution)/shard_map/ppermute | solution.py:437
  97.8 3.6 %collective-permute-start.12 = (f32[1,256]{1,0:T(1,128)S(1)}, f32[1,256]{1,0:T(1,128)S(1)}, u32[]{:S(2)}, u32[]{:S(2)}) collective-permute-start(f32[1,256]{1,0:T(1,128)S(1)} %add.80), channel_id=1, source_target_pairs={{0,2},{1,3},{2,0},{3,1},{4,6},{5,7},{6,4},{7,5},{8,10},{9,11},{10,... | collective-permute-start | bytes 3080 | tf_op jit(solution)/shard_map/ppermute | solution.py:437
  101.3 4.5 %collective-permute-start.15 = (f32[1,256]{1,0:T(1,128)S(1)}, f32[1,256]{1,0:T(1,128)S(1)}, u32[]{:S(2)}, u32[]{:S(2)}) collective-permute-start(f32[1,256]{1,0:T(1,128)S(1)} %add_add_fusion), channel_id=1, source_target_pairs={{0,8},{1,9},{2,10},{3,11},{4,12},{5,13},{6,14},{7,15},{8,0},{9,1},... | collective-permute-start | bytes 3080 | tf_op jit(solution)/shard_map/ppermute | solution.py:421

commit v4 on v2

--- a/solution.py
+++ b/solution.py
@@ -347,7 +347,7 @@
     for i in range(count):
         copies[i].wait()
         scale = a_ref[i : i + 1, :] * both
-        for at, size in chunks(depth, 192):
+        for at, size in chunks(depth, 288):
             high, low = split(x_ref[i, at : at + size, :])
             block = mul(high, halves[0])
             block = block + mul(low, halves[0])

time: 104 us -> 103 us (level)
  Pallas kernels: 42.7 us -> 40.7 us
    pallas_call x1, Pallas kernels: 10.1 us -> 8.11 us  [third_call(): pl.pallas_call(third_kernel, in_specs=[pl.BlockSpec(memory_space=pltpu.HB...]
  transfers between devices with their start and end apart: 14 -> 14, of which waited for: 13 -> 13; matrix products, arithmetic and copies ran while one was open for 1% -> 1% of each run, Pallas kernels for 17% -> 18%
where the time goes in v4:
time: 103 us; the launch traced here: 102 us
  Pallas kernels  40.7 us (40%)
  waiting for transfers between devices  30.5 us (30%)
  starting transfers between devices  24.7 us (24%)
  local copies, waits for them, and re-layouts  4.01 us (4%)
  other arithmetic  1.57 us (2%)
    pallas_call x1, Pallas kernels, first_call(): pl.pallas_call(first_kernel, in_specs=[pl.BlockSpec(memory_space=pltpu.HB...  14.4 us
    ppermute x6, waiting for transfers between devices, swap(): return lax.ppermute(x, 'gx', [(i, i ^ 1 << bit) for i in range(devices)])  13.6 us
    all_to_all x2, starting transfers between devices, exchange(): return lax.all_to_all(x, 'gx', 0, 0, axis_index_groups=groups, tiled=True)  11.3 us
    ppermute x6, waiting for transfers between devices, pass_to(): return lax.ppermute(x, 'gx', [(i, i ^ mask) for i in range(devices)])  9.67 us
    pallas_call x1, Pallas kernels, second_call(): pl.pallas_call(functools.partial(second_kernel, float(gathered.shape[0]))...  9.56 us
    pallas_call x1, Pallas kernels, fourth_call(): pl.pallas_call(fourth_kernel, out_shape=jax.ShapeDtypeStruct(gram_a.shape...  8.65 us
    pallas_call x1, Pallas kernels, third_call(): pl.pallas_call(third_kernel, in_specs=[pl.BlockSpec(memory_space=pltpu.HB...  8.11 us
    ppermute x6, starting transfers between devices, pass_to(): return lax.ppermute(x, 'gx', [(i, i ^ mask) for i in range(devices)])  8.1 us
  transfers between devices with their start and end apart: 14, of which 13 were waited for; matrix products, arithmetic and copies ran while one was open for 1% of the time, Pallas kernels for 18%

profile of v4, /device:TPU:0, one launch (start us, length us, event | category | flops | bytes accessed | tf_op | source)
XLA Modules:
  0.0 102.5 jit_solution(8062675588929738811)
XLA Ops:
  0.6 1.3 %copy-done = f32[1152,256]{1,0:T(8,128)S(1)} copy-done((f32[1152,256]{1,0:T(8,128)S(1)}, f32[1152,256]{1,0:T(8,128)}, u32[]{:S(2)}) %copy-start) | copy-done | bytes 1179672
  1.9 1.1 %copy-done.1 = f32[576,256]{1,0:T(8,128)S(1)} copy-done((f32[576,256]{1,0:T(8,128)S(1)}, f32[576,256]{1,0:T(8,128)}, u32[]{:S(2)}) %copy-start.1) | copy-done | bytes 589848
  3.0 14.4 %shard_map.58 = (f32[4,256]{1,0:T(4,128)S(1)}, f32[8,16,1280]{2,1,0:T(8,128)S(1)}, f32[8,16,1280]{2,1,0:T(8,128)S(1)}, f32[256,256]{1,0:T(8,128)S(1)}) custom-call(f32[4,576,1152]{2,1,0:T(8,128)} %bitcast.48, f32[1152,256]{1,0:T(8,128)S(1)} %copy-done, f32[576,256]{1,0:T(8,128)S(1)} %copy-done.1), custom_call_target="tpu_custom_call" | custom-call | flops 4076863488 | bytes 10616832 | tf_op jit(solution)/shard_map/pallas_call | solution.py:263
  17.4 0.5 collective-permute-start
  17.9 1.7 %collective-permute-done = f32[8,16,1280]{2,1,0:T(8,128)S(1)} collective-permute-done((f32[8,16,1280]{2,1,0:T(8,128)S(1)}, f32[8,16,1280]{2,1,0:T(8,128)S(1)}, u32[]{:S(2)}, u32[]{:S(2)}) %collective-permute-start) | collective-permute-done | bytes 655392 | tf_op jit(solution)/shard_map/ppermute | solution.py:421
  19.7 4.0 %collective-permute-start.3 = (f32[2,16,1280]{2,1,0:T(8,128)S(1)}, f32[2,16,1280]{2,1,0:T(8,128)S(1)}, u32[]{:S(2)}, u32[]{:S(2)}) collective-permute-start(f32[2,16,1280]{2,1,0:T(8,128)S(1)} %get-tuple-element.31), channel_id=1, source_target_pairs={{0,6},{1,7},{2,4},{3,5},{4,2},{5,3},{6,0},{7,1},{8,14},{9,15},{10,... | collective-permute-start | bytes 491528 | tf_op jit(solution)/shard_map/ppermute | solution.py:437
  24.4 4.3 %collective-permute-done.3 = f32[2,16,1280]{2,1,0:T(8,128)S(1)} collective-permute-done((f32[2,16,1280]{2,1,0:T(8,128)S(1)}, f32[2,16,1280]{2,1,0:T(8,128)S(1)}, u32[]{:S(2)}, u32[]{:S(2)}) %collective-permute-start.3) | collective-permute-done | bytes 163872 | tf_op jit(solution)/shard_map/ppermute | solution.py:437
  28.7 3.2 %collective-permute-done.2 = f32[2,16,1280]{2,1,0:T(8,128)S(1)} collective-permute-done((f32[2,16,1280]{2,1,0:T(8,128)S(1)}, f32[2,16,1280]{2,1,0:T(8,128)S(1)}, u32[]{:S(2)}, u32[]{:S(2)}) %collective-permute-start.2) | collective-permute-done | bytes 163872 | tf_op jit(solution)/shard_map/ppermute | solution.py:437
  32.1 2.7 %collective-permute-start.4 = (f32[1,16,1664]{2,1,0:T(8,128)S(1)}, f32[1,16,1664]{2,1,0:T(8,128)S(1)}, u32[]{:S(2)}, u32[]{:S(2)}) collective-permute-start(f32[1,16,1664]{2,1,0:T(8,128)S(1)} %pad_maximum_fusion), channel_id=1, source_target_pairs={{0,8},{1,9},{2,10},{3,11},{4,12},{5,13},{6,14},{7,15},{8,0},{9,1},... | collective-permute-start | bytes 319496 | tf_op jit(solution)/shard_map/ppermute | solution.py:421
  34.7 5.3 %collective-permute-done.4 = f32[1,16,1664]{2,1,0:T(8,128)S(1)} collective-permute-done((f32[1,16,1664]{2,1,0:T(8,128)S(1)}, f32[1,16,1664]{2,1,0:T(8,128)S(1)}, u32[]{:S(2)}, u32[]{:S(2)}) %collective-permute-start.4) | collective-permute-done | bytes 106528 | tf_op jit(solution)/shard_map/ppermute | solution.py:421
  40.0 0.9 broadcast_in_dim.11
  40.9 6.0 %all-to-all-start = ((f32[8,16,1152]{2,1,0:T(8,128)}), f32[8,16,1152]{2,1,0:T(8,128)S(1)}, u32[]{:S(2)}, u32[]{:S(2)}) async-start(f32[8,16,1152]{2,1,0:T(8,128)} %broadcast_in_dim.11), calls=%async_computation | async-start | bytes 1179648 | tf_op jit(solution)/shard_map/all_to_all | solution.py:425
  47.0 9.6 %shard_map.59 = (f32[4,256]{1,0:T(4,128)}, f32[1,256]{1,0:T(1,128)S(1)}, f32[256,256]{1,0:T(8,128)S(1)}, f32[256,256]{1,0:T(8,128)S(1)}) custom-call(f32[64,256]{1,0:T(8,128)S(1)} %bitcast.34, f32[4,256]{1,0:T(4,128)S(1)} %get-tuple-element.19.own_ref.a_ref, f32[256,256]{1,0:T(8,128)S(1)} %get-tuple-element.20.gram_c_ref), custom_call_target="tpu_custom_call" | custom-call | flops 10000000000 | bytes 1000000 | tf_op jit(solution)/shard_map/pallas_call | solution.py:314
  56.5 5.2 %all-to-all-done = f32[8,16,1152]{2,1,0:T(8,128)S(1)} async-done(((f32[8,16,1152]{2,1,0:T(8,128)}), f32[8,16,1152]{2,1,0:T(8,128)S(1)}, u32[]{:S(2)}, u32[]{:S(2)}) %all-to-all-start) | async-done | bytes 589856 | tf_op jit(solution)/shard_map/all_to_all | solution.py:425
  61.7 2.0 %collective-permute-done.5 = f32[8,16,1152]{2,1,0:T(8,128)S(1)} collective-permute-done((f32[8,16,1152]{2,1,0:T(8,128)S(1)}, f32[8,16,1152]{2,1,0:T(8,128)S(1)}, u32[]{:S(2)}, u32[]{:S(2)}) %collective-permute-start.5) | collective-permute-done | bytes 589856 | tf_op jit(solution)/shard_map/ppermute | solution.py:421
  63.7 8.1 %shard_map.60 = (f32[1152,256]{1,0:T(8,128)S(1)}, f32[256,256]{1,0:T(8,128)S(1)}, f32[8,40,256]{2,1,0:T(8,128)S(1)}, f32[8,40,256]{2,1,0:T(8,128)S(1)}) custom-call(f32[4,576,1152]{2,1,0:T(8,128)} %bitcast.49, f32[4,256]{1,0:T(4,128)S(1)} %get-tuple-element.19.own_ref.a_ref, f32[1,256]{1,0:T(1,128)S(1)} %get-tuple-element.22.scale_ref, ...), custom_call_target="tpu_custom_call" | custom-call | flops 4076863488 | bytes 10616832 | tf_op jit(solution)/shard_map/pallas_call | solution.py:380
  72.0 1.5 %collective-permute-done.6 = f32[8,40,256]{2,1,0:T(8,128)S(1)} collective-permute-done((f32[8,40,256]{2,1,0:T(8,128)S(1)}, f32[8,40,256]{2,1,0:T(8,128)S(1)}, u32[]{:S(2)}, u32[]{:S(2)}) %collective-permute-start.6) | collective-permute-done | bytes 327712 | tf_op jit(solution)/shard_map/ppermute | solution.py:421
  73.5 0.8 add.79
  74.3 5.3 %all-to-all-start.1 = ((f32[8,40,256]{2,1,0:T(8,128)}), f32[8,40,256]{2,1,0:T(8,128)S(1)}, u32[]{:S(2)}, u32[]{:S(2)}) async-start(f32[8,40,256]{2,1,0:T(8,128)} %add.79), calls=%async_computation.1 | async-start | bytes 655360 | tf_op jit(solution)/shard_map/all_to_all | solution.py:425
  79.7 8.6 %shard_map.61 = f32[256,256]{1,0:T(8,128)S(1)} custom-call(f32[256,256]{1,0:T(8,128)S(1)} %get-tuple-element.29.a_ref, f32[256,256]{1,0:T(8,128)S(1)} %get-tuple-element.30.b_ref), custom_call_target="tpu_custom_call" | custom-call | flops 10000000000 | bytes 1000000 | tf_op jit(solution)/shard_map/pallas_call | solution.py:411
  88.3 2.0 %all-to-all-done.1 = f32[8,40,256]{2,1,0:T(8,128)S(1)} async-done(((f32[8,40,256]{2,1,0:T(8,128)}), f32[8,40,256]{2,1,0:T(8,128)S(1)}, u32[]{:S(2)}, u32[]{:S(2)}) %all-to-all-start.1) | async-done | bytes 327712 | tf_op jit(solution)/shard_map/all_to_all | solution.py:425
  90.7 1.1 %collective-permute-done.7 = f32[1,256]{1,0:T(1,128)S(1)} collective-permute-done((f32[1,256]{1,0:T(1,128)S(1)}, f32[1,256]{1,0:T(1,128)S(1)}, u32[]{:S(2)}, u32[]{:S(2)}) %collective-permute-start.7) | collective-permute-done | bytes 1056 | tf_op jit(solution)/shard_map/ppermute | solution.py:421
  91.8 1.4 %collective-permute-start.10 = (f32[1,256]{1,0:T(1,128)S(1)}, f32[1,256]{1,0:T(1,128)S(1)}, u32[]{:S(2)}, u32[]{:S(2)}) collective-permute-start(f32[1,256]{1,0:T(1,128)S(1)} %add.80), channel_id=1, source_target_pairs={{0,6},{1,7},{2,4},{3,5},{4,2},{5,3},{6,0},{7,1},{8,14},{9,15},{10,... | collective-permute-start | bytes 3080 | tf_op jit(solution)/shard_map/ppermute | solution.py:437
  93.2 0.6 collective-permute-start.9
  93.8 1.5 %collective-permute-start.8 = (f32[1,256]{1,0:T(1,128)S(1)}, f32[1,256]{1,0:T(1,128)S(1)}, u32[]{:S(2)}, u32[]{:S(2)}) collective-permute-start(f32[1,256]{1,0:T(1,128)S(1)} %add.80), channel_id=1, source_target_pairs={{0,2},{1,3},{2,0},{3,1},{4,6},{5,7},{6,4},{7,5},{8,10},{9,11},{10,... | collective-permute-start | bytes 3080 | tf_op jit(solution)/shard_map/ppermute | solution.py:437
  95.3 1.0 collective-permute-done.10
  96.3 0.5 collective-permute-done.9
  96.8 0.6 collective-permute-done.8
  97.4 1.8 %collective-permute-start.11 = (f32[1,256]{1,0:T(1,128)S(1)}, f32[1,256]{1,0:T(1,128)S(1)}, u32[]{:S(2)}, u32[]{:S(2)}) collective-permute-start(f32[1,256]{1,0:T(1,128)S(1)} %add_add_fusion), channel_id=1, source_target_pairs={{0,8},{1,9},{2,10},{3,11},{4,12},{5,13},{6,14},{7,15},{8,0},{9,1},... | collective-permute-start | bytes 3080 | tf_op jit(solution)/shard_map/ppermute | solution.py:421
  99.2 0.6 constant_dynamic-slice_fusion
  99.9 2.0 %collective-permute-done.11 = f32[1,256]{1,0:T(1,128)S(1)} collective-permute-done((f32[1,256]{1,0:T(1,128)S(1)}, f32[1,256]{1,0:T(1,128)S(1)}, u32[]{:S(2)}, u32[]{:S(2)}) %collective-permute-start.11) | collective-permute-done | bytes 1056 | tf_op jit(solution)/shard_map/ppermute | solution.py:421
  101.9 0.6 broadcast_multiply_fusion
  (35 shorter events, 1.5 us)
Async XLA Ops:
  0.6 1.3 %copy-start = (f32[1152,256]{1,0:T(8,128)S(1)}, f32[1152,256]{1,0:T(8,128)}, u32[]{:S(2)}) copy-start(f32[1152,256]{1,0:T(8,128)} %b_ref.1) | copy-start | bytes 3538948
  1.9 1.1 %copy-start.1 = (f32[576,256]{1,0:T(8,128)S(1)}, f32[576,256]{1,0:T(8,128)}, u32[]{:S(2)}) copy-start(f32[576,256]{1,0:T(8,128)} %c_ref.1) | copy-start | bytes 1769476
  17.4 2.2 %collective-permute-start = (f32[8,16,1280]{2,1,0:T(8,128)S(1)}, f32[8,16,1280]{2,1,0:T(8,128)S(1)}, u32[]{:S(2)}, u32[]{:S(2)}) collective-permute-start(f32[8,16,1280]{2,1,0:T(8,128)S(1)} %get-tuple-element.18), channel_id=1, source_target_pairs={{0,1},{1,0},{2,3},{3,2},{4,5},{5,4},{6,7},{7,6},{8,9},{9,8},{10,11... | collective-permute-start | bytes 1966088 | tf_op jit(solution)/shard_map/ppermute | solution.py:421
  19.7 9.0 %collective-permute-start.3 = (f32[2,16,1280]{2,1,0:T(8,128)S(1)}, f32[2,16,1280]{2,1,0:T(8,128)S(1)}, u32[]{:S(2)}, u32[]{:S(2)}) collective-permute-start(f32[2,16,1280]{2,1,0:T(8,128)S(1)} %get-tuple-element.31), channel_id=1, source_target_pairs={{0,6},{1,7},{2,4},{3,5},{4,2},{5,3},{6,0},{7,1},{8,14},{9,15},{10,... | collective-permute-start | bytes 491528 | tf_op jit(solution)/shard_map/ppermute | solution.py:437
  23.7 8.2 %collective-permute-start.2 = (f32[2,16,1280]{2,1,0:T(8,128)S(1)}, f32[2,16,1280]{2,1,0:T(8,128)S(1)}, u32[]{:S(2)}, u32[]{:S(2)}) collective-permute-start(f32[2,16,1280]{2,1,0:T(8,128)S(1)} %get-tuple-element.32), channel_id=1, source_target_pairs={{0,4},{1,5},{2,6},{3,7},{4,0},{5,1},{6,2},{7,3},{8,12},{9,13},{10,... | collective-permute-start | bytes 491528 | tf_op jit(solution)/shard_map/ppermute | solution.py:437
  24.2 7.8 %collective-permute-start.1 = (f32[2,16,1280]{2,1,0:T(8,128)S(1)}, f32[2,16,1280]{2,1,0:T(8,128)S(1)}, u32[]{:S(2)}, u32[]{:S(2)}) collective-permute-start(f32[2,16,1280]{2,1,0:T(8,128)S(1)} %get-tuple-element.33), channel_id=1, source_target_pairs={{0,2},{1,3},{2,0},{3,1},{4,6},{5,7},{6,4},{7,5},{8,10},{9,11},{10,... | collective-permute-start | bytes 491528 | tf_op jit(solution)/shard_map/ppermute | solution.py:437
  32.1 8.0 %collective-permute-start.4 = (f32[1,16,1664]{2,1,0:T(8,128)S(1)}, f32[1,16,1664]{2,1,0:T(8,128)S(1)}, u32[]{:S(2)}, u32[]{:S(2)}) collective-permute-start(f32[1,16,1664]{2,1,0:T(8,128)S(1)} %pad_maximum_fusion), channel_id=1, source_target_pairs={{0,8},{1,9},{2,10},{3,11},{4,12},{5,13},{6,14},{7,15},{8,0},{9,1},... | collective-permute-start | bytes 319496 | tf_op jit(solution)/shard_map/ppermute | solution.py:421
  40.9 20.8 %all-to-all-start = ((f32[8,16,1152]{2,1,0:T(8,128)}), f32[8,16,1152]{2,1,0:T(8,128)S(1)}, u32[]{:S(2)}, u32[]{:S(2)}) async-start(f32[8,16,1152]{2,1,0:T(8,128)} %broadcast_in_dim.11), calls=%async_computation | async-start | bytes 1179648 | tf_op jit(solution)/shard_map/all_to_all | solution.py:425
  61.7 2.0 %collective-permute-start.5 = (f32[8,16,1152]{2,1,0:T(8,128)S(1)}, f32[8,16,1152]{2,1,0:T(8,128)S(1)}, u32[]{:S(2)}, u32[]{:S(2)}) collective-permute-start(f32[8,16,1152]{2,1,0:T(8,128)S(1)} %all-to-all-done), channel_id=1, source_target_pairs={{0,1},{1,0},{2,3},{3,2},{4,5},{5,4},{6,7},{7,6},{8,9},{9,8},{10,11... | collective-permute-start | bytes 1769480 | tf_op jit(solution)/shard_map/ppermute | solution.py:421
  71.9 1.7 %collective-permute-start.6 = (f32[8,40,256]{2,1,0:T(8,128)S(1)}, f32[8,40,256]{2,1,0:T(8,128)S(1)}, u32[]{:S(2)}, u32[]{:S(2)}) collective-permute-start(f32[8,40,256]{2,1,0:T(8,128)S(1)} %get-tuple-element.28), channel_id=1, source_target_pairs={{0,1},{1,0},{2,3},{3,2},{4,5},{5,4},{6,7},{7,6},{8,9},{9,8},{10,11... | collective-permute-start | bytes 983048 | tf_op jit(solution)/shard_map/ppermute | solution.py:421
  74.3 16.0 %all-to-all-start.1 = ((f32[8,40,256]{2,1,0:T(8,128)}), f32[8,40,256]{2,1,0:T(8,128)S(1)}, u32[]{:S(2)}, u32[]{:S(2)}) async-start(f32[8,40,256]{2,1,0:T(8,128)} %add.79), calls=%async_computation.1 | async-start | bytes 655360 | tf_op jit(solution)/shard_map/all_to_all | solution.py:425
  90.6 1.2 %collective-permute-start.7 = (f32[1,256]{1,0:T(1,128)S(1)}, f32[1,256]{1,0:T(1,128)S(1)}, u32[]{:S(2)}, u32[]{:S(2)}) collective-permute-start(f32[1,256]{1,0:T(1,128)S(1)} %bitcast.45), channel_id=1, source_target_pairs={{0,1},{1,0},{2,3},{3,2},{4,5},{5,4},{6,7},{7,6},{8,9},{9,8},{10,11... | collective-permute-start | bytes 3080 | tf_op jit(solution)/shard_map/ppermute | solution.py:421
  91.8 4.5 %collective-permute-start.10 = (f32[1,256]{1,0:T(1,128)S(1)}, f32[1,256]{1,0:T(1,128)S(1)}, u32[]{:S(2)}, u32[]{:S(2)}) collective-permute-start(f32[1,256]{1,0:T(1,128)S(1)} %add.80), channel_id=1, source_target_pairs={{0,6},{1,7},{2,4},{3,5},{4,2},{5,3},{6,0},{7,1},{8,14},{9,15},{10,... | collective-permute-start | bytes 3080 | tf_op jit(solution)/shard_map/ppermute | solution.py:437
  93.2 3.6 %collective-permute-start.9 = (f32[1,256]{1,0:T(1,128)S(1)}, f32[1,256]{1,0:T(1,128)S(1)}, u32[]{:S(2)}, u32[]{:S(2)}) collective-permute-start(f32[1,256]{1,0:T(1,128)S(1)} %add.80), channel_id=1, source_target_pairs={{0,4},{1,5},{2,6},{3,7},{4,0},{5,1},{6,2},{7,3},{8,12},{9,13},{10,... | collective-permute-start | bytes 3080 | tf_op jit(solution)/shard_map/ppermute | solution.py:437
  93.8 3.6 %collective-permute-start.8 = (f32[1,256]{1,0:T(1,128)S(1)}, f32[1,256]{1,0:T(1,128)S(1)}, u32[]{:S(2)}, u32[]{:S(2)}) collective-permute-start(f32[1,256]{1,0:T(1,128)S(1)} %add.80), channel_id=1, source_target_pairs={{0,2},{1,3},{2,0},{3,1},{4,6},{5,7},{6,4},{7,5},{8,10},{9,11},{10,... | collective-permute-start | bytes 3080 | tf_op jit(solution)/shard_map/ppermute | solution.py:437
  97.4 4.5 %collective-permute-start.11 = (f32[1,256]{1,0:T(1,128)S(1)}, f32[1,256]{1,0:T(1,128)S(1)}, u32[]{:S(2)}, u32[]{:S(2)}) collective-permute-start(f32[1,256]{1,0:T(1,128)S(1)} %add_add_fusion), channel_id=1, source_target_pairs={{0,8},{1,9},{2,10},{3,11},{4,12},{5,13},{6,14},{7,15},{8,0},{9,1},... | collective-permute-start | bytes 3080 | tf_op jit(solution)/shard_map/ppermute | solution.py:421
